TPU v7x, 128 devices: a whole 4x4x4 slice. The times are simulated.
128 devices in a mesh: ctx: 32 (over z, y, core), exp: 4 (over x).
Axes of the slice: x: 4, y: 4, z: 4, core: 2. Of those that a mesh axis runs over, the one named last changes fastest.
Arguments:
- tokens: bfloat16 [4096, 4096], P('ctx'), may hold values from -6 to 6
- ada_shift: float32 [4096], replicated, may hold values from -3 to 3
- ada_scale: float32 [4096], replicated, may hold values from -3 to 3
- ada_gate: float32 [4096], replicated, may hold values from -6 to 6
- router: bfloat16 [4, 4096, 2], P('exp'), may hold values from -0.09375 to 0.09375
- expert_up: bfloat16 [4, 4096, 16384], P('exp', None, 'ctx'), may hold values from -0.09375 to 0.09375
- expert_down: bfloat16 [4, 16384, 4096], P('exp', 'ctx'), may hold values from -0.0625 to 0.0625
- picked_ids: int32 [4, 2, 128], P('exp'), may hold values from 0 to 4095, as said below
- out_grad: bfloat16 [4096, 4096], P('ctx'), may hold values from -6 to 6
Outputs:
- block_out: bfloat16 [4096, 4096], P('ctx')
- tokens_grad: bfloat16 [4096, 4096], P('ctx')
- up_grad: bfloat16 [4, 4096, 16384], P('exp', None, 'ctx')
- down_grad: bfloat16 [4, 16384, 4096], P('exp', 'ctx')
- router_grad: float32 [4, 4096, 2], P('exp')
- shift_grad: float32 [4096], replicated
- scale_grad: float32 [4096], replicated
- gate_grad: float32 [4096], replicated
Inputs may be any that keep to these rules, and one draw needn't show every extreme that they name: Row picked_ids[e, j] lists 128 distinct tokens for expert e * 2 + j. Among the 128 tokens of any one index of ctx it picks at most 8, and for each expert exactly 8 from at least one such index.
All inputs are finite; a program needn't handle non-finite values.
Results may differ from a plain program's by a relative error of at most 0.007.
Values may be sent and summed in bfloat16 or wider, within the bound.
A program may use at most 128 MiB of HBM per device.

v0:
```python
import jax
import jax.numpy as jnp
from jax import lax
from jax.sharding import PartitionSpec as P

MOST = 8


GELU_C = 0.7978845608028654


def gelu_tanh(values):
    inner_arg = GELU_C * (values + 0.044715 * values * values * values)
    return 0.5 * values * (1.0 + jnp.tanh(inner_arg))


def gelu_slope(values):
    inner_arg = GELU_C * (values + 0.044715 * values * values * values)
    tangent = jnp.tanh(inner_arg)
    return 0.5 * (1.0 + tangent) + 0.5 * values * (1.0 - tangent * tangent) * GELU_C * (
        1.0 + 3.0 * 0.044715 * values * values
    )


def select_table(token_ids, start_row, tok_count, most_rows):
    local_ids = token_ids - start_row
    inside = (local_ids >= 0) & (local_ids < tok_count)
    position = jnp.cumsum(inside.astype(jnp.int32)) - 1
    slot_hit = (position[:, None] == jnp.arange(most_rows, dtype=jnp.int32)[None, :]) & inside[
        :, None
    ]
    token_hit = local_ids[:, None] == jnp.arange(tok_count, dtype=jnp.int32)[None, :]
    return lax.dot_general(
        slot_hit.astype(jnp.float32),
        token_hit.astype(jnp.float32),
        (((0,), (0,)), ((), ())),
        precision=lax.Precision.HIGHEST,
    )


def sum_experts(values):
    return lax.psum(values, "exp")


def per_device(
    tokens, ada_shift, ada_scale, ada_gate, router, expert_up, expert_down, picked_ids, out_grad
):
    highest = lax.Precision.HIGHEST
    tok_count = tokens.shape[0]
    width = tokens.shape[1]
    pair_count = picked_ids.shape[1]
    ctx_size = lax.axis_size("ctx")
    members = ctx_size // pair_count
    ctx_place = lax.axis_index("ctx")
    my_group = ctx_place // members
    start_row = ctx_place * tok_count
    tables = jnp.stack(
        [
            select_table(picked_ids[0, slot_index], start_row, tok_count, MOST)
            for slot_index in range(pair_count)
        ]
    )

    def deliver(row_data):
        everyone = lax.all_gather(row_data, "ctx", axis=0, tiled=True)
        everyone = everyone.reshape(ctx_size, pair_count, MOST, width)
        chosen = lax.dynamic_index_in_dim(everyone, my_group, 1, keepdims=False)
        return chosen.reshape(ctx_size * MOST, width)

    def send_back(left, product):
        group_mask = (jnp.arange(pair_count, dtype=jnp.int32) == my_group).astype(jnp.float32)[
            None, :, None, None
        ]
        dest_count = pair_count * MOST * lax.axis_size("ctx") // (pair_count * MOST)
        product_rows = product(left).reshape(dest_count, 1, MOST, width)
        summed = lax.psum_scatter(
            (product_rows * group_mask).reshape(pair_count * MOST * lax.axis_size("ctx"), width),
            "ctx",
            scatter_dimension=0,
            tiled=True,
        )
        return summed.reshape(pair_count, MOST, width)

    inputs = tokens.astype(jnp.float32)
    centered = inputs - jnp.mean(inputs, axis=1, keepdims=True)
    inverse_std = lax.rsqrt(jnp.mean(centered * centered, axis=1, keepdims=True) + 1e-06)
    normed = centered * inverse_std
    hidden = (normed * (1.0 + ada_scale) + ada_shift).astype(jnp.bfloat16)
    router_cols = router[0]
    logits = jnp.dot(hidden, router_cols, preferred_element_type=jnp.float32)
    weights = jax.nn.sigmoid(logits)
    row_weight = jnp.einsum("jmt,tj->jm", tables, weights, precision=highest)
    sent_rows = jnp.einsum(
        "jmt,td->jmd", tables.astype(jnp.bfloat16), hidden, preferred_element_type=jnp.float32
    ).astype(jnp.bfloat16)
    up_slice = expert_up[0]
    down_slice = expert_down[0]
    expert_rows = deliver(sent_rows)
    pre_act = jnp.dot(expert_rows, up_slice, preferred_element_type=jnp.float32)
    activated = gelu_tanh(pre_act).astype(jnp.bfloat16)

    def down_product(row_block):
        return jnp.dot(row_block, down_slice, preferred_element_type=jnp.float32)

    expert_out = send_back(activated, down_product)
    contrib = jnp.einsum(
        "jmt,jmd->td", tables, row_weight[:, :, None] * expert_out, precision=highest
    )
    mixture = sum_experts(contrib)
    block_out = (inputs + ada_gate * mixture).astype(jnp.bfloat16)
    grad_in = out_grad.astype(jnp.float32)
    grad_mix = ada_gate * grad_in
    mix_rows = jnp.einsum("jmt,td->jmd", tables, grad_mix, precision=highest)
    grad_rows = (row_weight[:, :, None] * mix_rows).astype(jnp.bfloat16)
    grad_weight = jnp.sum(mix_rows * expert_out, axis=2)
    grad_logit = grad_weight * row_weight * (1.0 - row_weight)
    logit_tok = jnp.einsum("jmt,jm->tj", tables, grad_logit, precision=highest)
    expert_grads = deliver(grad_rows)
    grad_act = lax.dot_general(
        expert_grads, down_slice, (((1,), (1,)), ((), ())), preferred_element_type=jnp.float32
    )
    grad_pre = (grad_act * gelu_slope(pre_act)).astype(jnp.bfloat16)
    down_grad = lax.dot_general(
        activated, expert_grads, (((0,), (0,)), ((), ())), preferred_element_type=jnp.float32
    ).astype(jnp.bfloat16)
    up_grad = lax.dot_general(
        expert_rows, grad_pre, (((0,), (0,)), ((), ())), preferred_element_type=jnp.float32
    ).astype(jnp.bfloat16)

    def up_product(row_block):
        return lax.dot_general(
            row_block, up_slice, (((1,), (1,)), ((), ())), preferred_element_type=jnp.float32
        )

    back_rows = send_back(grad_pre, up_product)
    grad_local = jnp.einsum("jmt,jmd->td", tables, back_rows, precision=highest)
    grad_local = grad_local + lax.dot_general(
        logit_tok, router_cols.astype(jnp.float32), (((1,), (1,)), ((), ())), precision=highest
    )
    grad_hidden = sum_experts(grad_local)
    grad_norm = grad_hidden * (1.0 + ada_scale)
    tokens_grad = (
        grad_in
        + inverse_std
        * (
            grad_norm
            - jnp.mean(grad_norm, axis=1, keepdims=True)
            - normed * jnp.mean(grad_norm * normed, axis=1, keepdims=True)
        )
    ).astype(jnp.bfloat16)
    router_part = lax.dot_general(
        hidden.astype(jnp.float32), logit_tok, (((0,), (0,)), ((), ())), precision=highest
    )
    vectors = jnp.stack(
        [
            jnp.sum(grad_hidden, axis=0),
            jnp.sum(grad_hidden * normed, axis=0),
            jnp.sum(grad_in * mixture, axis=0),
        ]
    )
    router_total, vector_total = lax.psum((router_part, vectors), "ctx")
    return (
        block_out,
        tokens_grad,
        up_grad[None],
        down_grad[None],
        router_total[None],
        vector_total[0],
        vector_total[1],
        vector_total[2],
    )


def solution(mesh):
    in_specs = (
        P("ctx", None),
        P(),
        P(),
        P(),
        P("exp", None, None),
        P("exp", None, "ctx"),
        P("exp", "ctx", None),
        P("exp", None, None),
        P("ctx", None),
    )
    out_specs = (
        P("ctx", None),
        P("ctx", None),
        P("exp", None, "ctx"),
        P("exp", "ctx", None),
        P("exp", None, None),
        P(),
        P(),
        P(),
    )
    return jax.shard_map(
        per_device, mesh=mesh, in_specs=in_specs, out_specs=out_specs, check_vma=False
    )
```

profile of v0, /device:TPU:1, one launch (start us, length us, event | category | flops | bytes accessed | tf_op | source)
XLA Modules:
  0.0 531.6 jit_solution(10288617940273825963)
XLA Ops:
  7.3 0.8 fusion.77
  8.0 0.8 compare_and_fusion.1
  8.8 0.8 fusion.89
  10.4 1.5 convert_reduce_fusion
  12.8 0.5 fusion.17
  13.3 0.9 convolution_convert_fusion.2
  14.5 49.9 %all-gather.3.cloned.1.call-done = bf16[64,8,4096]{2,1,0:T(8,128)(2,1)} async-done(((bf16[2,8,4096]{2,1,0:T(8,128)(2,1)}), bf16[64,8,4096]{2,1,0:T(8,128)(2,1)}) %all-gather.3.cloned.1.call-update) | async-done | bytes 4194320 | tf_op jit(solution)/shard_map/all_gather | solution.py:65
  64.4 4.2 fusion.8
  68.7 0.8 copy-done.6
  69.4 1.3 fusion.4
  70.8 4.5 bitcast_multiply_fusion.1
  75.9 89.6 %reduce-scatter.3.cloned.1.call-done = f32[16,4096]{1,0:T(8,128)} async-done(((f32[512,4096]{1,0:T(8,128)}), f32[16,4096]{1,0:T(8,128)}) %reduce-scatter.3.cloned.1.call-update) | async-done | bytes 262160 | tf_op jit(solution)/shard_map/reduce_scatter | solution.py:76
  165.5 2.8 fusion.59
  168.4 47.9 %all-gather.5.cloned.1.call-done = bf16[64,8,4096]{2,1,0:T(8,128)(2,1)} async-done(((bf16[2,8,4096]{2,1,0:T(8,128)(2,1)}), bf16[64,8,4096]{2,1,0:T(8,128)(2,1)}) %all-gather.5.cloned.1.call-update) | async-done | bytes 4194320 | tf_op jit(solution)/shard_map/all_gather | solution.py:65
  216.3 4.5 fusion.42
  220.9 1.3 fusion.2
  222.2 4.5 bitcast_multiply_fusion
  226.9 0.7 copy-done.7
  227.6 3.2 convolution_bitcast_fusion.1
  230.9 86.0 %reduce-scatter.5.cloned.1.call-done = f32[16,4096]{1,0:T(8,128)} async-done(((f32[512,4096]{1,0:T(8,128)}), f32[16,4096]{1,0:T(8,128)}) %reduce-scatter.5.cloned.1.call-update) | async-done | bytes 262160 | tf_op jit(solution)/shard_map/reduce_scatter | solution.py:76
  316.9 2.8 convolution_bitcast_fusion
  319.7 2.4 convolution_add_fusion
  322.1 1.1 convolution_bitcast_fusion.2
  323.3 5.1 fusion.1
  328.4 87.6 %all-reduce.7.cloned.1.call-done = (f32[128,4096]{1,0:T(8,128)}, f32[128,4096]{1,0:T(8,128)}) async-done(((f32[128,4096]{1,0:T(8,128)}, f32[128,4096]{1,0:T(8,128)}), (f32[128,4096]{1,0:T(8,128)}, f32[128,4096]{1,0:T(8,128)})) %all-reduce.7.cloned.1.call-update) | async-done | bytes 4194320 | tf_op jit(solution)/shard_map/psum | solution.py:42
  416.1 2.7 fusion.21
  418.8 4.3 fusion.28
  423.1 0.7 pad_maximum_fusion
  423.8 4.9 fusion
  428.7 93.0 %all-reduce.5.cloned.1.call-done = (f32[1,4096,2]{1,2,0:T(2,128)}, f32[3,4096]{1,0:T(4,128)}) async-done(((f32[1,4096,2]{1,2,0:T(2,128)}, f32[3,4096]{1,0:T(4,128)}), (f32[1,4096,2]{1,2,0:T(2,128)}, f32[3,4096]{1,0:T(4,128)})) %all-reduce.5.cloned.1.call-update) | async-done | bytes 81936 | tf_op jit(solution)/shard_map/psum | solution.py:161
  521.8 1.6 fusion.91
  523.4 1.4 copy.31
  (56 shorter events, 3.2 us)
Async XLA Ops:
  7.2 68.2 %copy-start = (bf16[1,4096,2]{1,2,0:T(2,128)(2,1)S(1)}, bf16[1,4096,2]{1,2,0:T(2,128)(2,1)}, u32[]{:S(2)}) copy-start(bf16[1,4096,2]{1,2,0:T(2,128)(2,1)} %param.13) | copy-start | bytes 49156
  7.2 4.6 copy-start.1
  7.2 5.1 copy-start.12
  7.2 5.6 %copy-start.11 = (f32[4096]{0:T(1024)S(1)}, f32[4096]{0:T(1024)}, u32[]{:S(2)}) copy-start(f32[4096]{0:T(1024)} %param.10) | copy-start | bytes 49156
  7.2 57.2 %all-gather.3.cloned.1.call-start = ((), (), s32[]{:S(2)}) async-start(), calls=%async_computation.2 | async-start | bytes 4325376 | tf_op jit(solution)/shard_map/all_gather | solution.py:65
  14.2 151.3 %reduce-scatter.3.cloned.1.call-start = ((), (), s32[]{:S(2)}) async-start(), calls=%async_computation.3 | async-start | bytes 8650752 | tf_op jit(solution)/shard_map/reduce_scatter | solution.py:76
  64.4 5.0 copy-start.4
  68.6 0.8 copy-start.6
  75.3 90.2 %copy-start.3 = (bf16[128,4096]{1,0:T(8,128)(2,1)S(1)}, bf16[128,4096]{1,0:T(8,128)(2,1)}, u32[]{:S(2)}) copy-start(bf16[128,4096]{1,0:T(8,128)(2,1)} %param.17) | copy-start | bytes 3145732
  75.3 90.2 %copy-start.10 = (f32[4096]{0:T(1024)S(1)}, f32[4096]{0:T(1024)}, u32[]{:S(2)}) copy-start(f32[4096]{0:T(1024)} %param.12) | copy-start | bytes 49156
  75.3 141.0 %all-gather.5.cloned.1.call-start = ((), (), s32[]{:S(2)}) async-start(), calls=%async_computation.4 | async-start | bytes 4325376 | tf_op jit(solution)/shard_map/all_gather | solution.py:65
  168.3 148.5 %reduce-scatter.5.cloned.1.call-start = ((), (), s32[]{:S(2)}) async-start(), calls=%async_computation.5 | async-start | bytes 8650752 | tf_op jit(solution)/shard_map/reduce_scatter | solution.py:76
  216.3 4.5 copy-start.5
  220.9 1.3 copy-start.8
  226.7 0.9 copy-start.7
  226.7 189.4 %all-reduce.7.cloned.1.call-start = ((), (), s32[]{:S(2)}) async-start(), calls=%async_computation.7 | async-start | bytes 8388608 | tf_op jit(solution)/shard_map/psum | solution.py:42
  322.1 199.7 %all-reduce.5.cloned.1.call-start = ((), (), s32[]{:S(2)}) async-start(), calls=%async_computation.6 | async-start | bytes 196608 | tf_op jit(solution)/shard_map/psum | solution.py:161
  416.1 2.7 copy-start.2
  418.8 5.0 copy-start.9
Sparse Core Ops, SparseCore 0:
  14.3 50.0 all-gather.2
  75.4 90.0 reduce-scatter.2
  168.6 47.6 all-gather.4
  226.8 90.0 reduce-scatter.4
  322.2 93.8 all-reduce.6
  423.9 97.7 all-reduce.4
where the time goes:
time: 532 us
  waiting for transfers between devices  454 us (85%)
  matrix products  35.8 us (7%)
  other arithmetic  21.9 us (4%)
  between operations  14.3 us (3%)
    reduce_scatter x2, waiting for transfers between devices, send_back(): lax.psum_scatter((product_rows * group_mask).reshape(pair_count * MOST *...  176 us
    all_gather x2, waiting for transfers between devices, deliver(): everyone = lax.all_gather(row_data, 'ctx', axis=0, tiled=True)  97.9 us
    psum x1, waiting for transfers between devices, per_device(): router_total, vector_total = lax.psum((router_part, vectors), 'ctx')  93 us
    psum x1, waiting for transfers between devices, sum_experts(): return lax.psum(values, 'exp')  87.6 us
  transfers between devices with their start and end apart: 6, of which 6 were waited for; matrix products, arithmetic and copies ran while one was open for 3% of the time, Pallas kernels for 0%

commit v1 on v0

v1 whole, which is shorter than its diff:
```python
import jax
import jax.numpy as jnp
from jax import lax
from jax.experimental import pallas as pl
from jax.experimental.pallas import tpu as pltpu
from jax.sharding import PartitionSpec as P

GELU_C = 0.7978845608028654
MESH = pl.DeviceIdType.MESH
F32 = jnp.float32
BF16 = jnp.bfloat16

D = 4096
HU = 512
TOK = 128
MOST = 8
NF = 2
F = D // NF
TILE = 512
SLOTS = 32 * MOST


def dot(a, b, ca, cb):
    return lax.dot_general(a, b, (((ca,), (cb,)), ((), ())), preferred_element_type=F32)


def exchange_kernel(
    tok_hbm,
    og_hbm,
    shift_ref,
    scale_ref,
    gate_ref,
    router_ref,
    up_hbm,
    down_hbm,
    picks_ref,
    block_hbm,
    tgrad_hbm,
    rows_hbm,
    grads_hbm,
    act_hbm,
    gp_hbm,
    vec_ref,
    tok,
    og,
    up,
    down,
    own,
    got,
    relay,
    rowmat,
    pre,
    gact,
    act,
    gpre,
    part,
    swap,
    first,
    mid,
    second,
    fin,
    slots,
    tables,
    mix,
    hid16,
    n64,
    og64,
    g64,
    c64,
    outb,
    outt,
    vparts,
    vin,
    vsum,
    gvec,
    loc,
    tab_s,
    tab_r,
    a1s,
    a1r,
    a2s,
    a2r,
    acs,
    acr,
    bcs,
    bcr,
    b1s,
    b1r,
    b2s,
    b2r,
    xs,
    xr,
    v1s,
    v1r,
    v2s,
    v2r,
):
    me = lax.axis_index("ctx")
    x = lax.axis_index("exp")
    z, y, c = me // 8, (me // 2) % 4, me % 2
    oc = 1 - c
    j = z // 2
    jo = 1 - j
    mate = (1 - z % 2) * 2

    def dev(zz, yy, cc, xx):
        return ((zz * 4 + yy) * 2 + cc, xx)

    def nxt(v, k):
        return (v + k) % 4

    pending = []

    def send(src, dst, ss, rs, to):
        cp = pltpu.make_async_remote_copy(
            src_ref=src, dst_ref=dst, send_sem=ss, recv_sem=rs, device_id=to, device_id_type=MESH
        )
        cp.start()
        pending.append(cp)
        return cp

    def local(src, dst, sem):
        cp = pltpu.make_async_copy(src, dst, sem)
        cp.start()
        return cp

    in_tok = local(tok_hbm, tok, loc.at[0])
    in_og = local(og_hbm, og, loc.at[1])
    in_up = local(up_hbm.at[0], up, loc.at[2])
    in_down = local(down_hbm.at[0], down, loc.at[3])

    bar = pltpu.get_barrier_semaphore()
    for k in range(1, 32):
        pl.semaphore_signal(bar, inc=1, device_id=((me + k) % 32, x), device_id_type=MESH)
    for k in range(1, 4):
        pl.semaphore_signal(bar, inc=1, device_id=(me, nxt(x, k)), device_id_type=MESH)

    lanes = lax.broadcasted_iota(jnp.int32, (MOST, TOK), 1)
    subl = lax.broadcasted_iota(jnp.int32, (MOST, TOK), 0)
    tri = (
        lax.broadcasted_iota(jnp.int32, (TOK, TOK), 0) <= lax.broadcasted_iota(jnp.int32, (TOK, TOK), 1)
    ).astype(F32).astype(BF16)
    tabs = []
    for jj in range(2):
        ids = jnp.broadcast_to(picks_ref[jj : jj + 1, :], (MOST, TOK)) - me * TOK
        inside = (ids >= 0) & (ids < TOK)
        inside_f = jnp.where(inside, 1.0, 0.0)
        count = dot(inside_f.astype(BF16), tri, 1, 0)
        hit = jnp.where(inside & (count == (subl + 1).astype(F32)), 1.0, 0.0)
        where_tok = jnp.sum(hit * ids.astype(F32), axis=1, keepdims=True)
        there = jnp.sum(hit, axis=1, keepdims=True)
        tabs.append(jnp.where((where_tok == lanes.astype(F32)) & (there > 0.5), 1.0, 0.0))
    table = jnp.concatenate(tabs, axis=0).astype(BF16)
    tables[x] = table

    in_tok.wait()
    trow = dot(table, tok[...], 1, 0)
    cen = trow - jnp.mean(trow, axis=1, keepdims=True)
    inv = lax.rsqrt(jnp.mean(cen * cen, axis=1, keepdims=True) + 1e-06)
    row_there = jnp.sum(table.astype(F32), axis=1, keepdims=True)
    hid = ((cen * inv * (1.0 + scale_ref[...]) + shift_ref[...]) * row_there).astype(BF16)
    hid16[...] = hid
    hidf = hid.astype(F32)
    rout = router_ref[...].astype(F32)
    logits = jnp.concatenate(
        [
            jnp.sum(hidf[MOST * jj : MOST * jj + MOST] * rout[jj : jj + 1], axis=1, keepdims=True)
            for jj in range(2)
        ],
        axis=0,
    )
    weight = 1.0 / (1.0 + jnp.exp(-logits))
    for f in range(NF):
        for jj in range(2):
            own[0, f, jj] = hidf[MOST * jj : MOST * jj + MOST, f * F : f * F + F].astype(BF16)
    in_og.wait()
    mixv = dot(table, og[...], 1, 0) * gate_ref[...]
    mix[...] = mixv
    gradv = weight * mixv
    for f in range(NF):
        for jj in range(2):
            own[1, f, jj] = gradv[MOST * jj : MOST * jj + MOST, f * F : f * F + F].astype(BF16)

    pl.semaphore_wait(bar, 34)

    tabc = [
        send(tables.at[x], tables.at[x], tab_s.at[k - 1], tab_r.at[k - 1], (me, nxt(x, k)))
        for k in range(1, 4)
    ]

    def recv(cps):
        for cp in cps:
            cp.wait_recv()

    def zfirst(f):
        return f % 2 == 0

    def gather1(a, f):
        if zfirst(f):
            return [
                send(
                    own.at[a, f, nxt(z, k) // 2],
                    got.at[a, f, c, y, z],
                    a1s.at[a, f, k - 1],
                    a1r.at[a, f, k - 1],
                    dev(nxt(z, k), y, c, x),
                )
                for k in range(1, 4)
            ]
        return [
            send(
                own.at[a, f],
                relay.at[a, f // 2, y],
                a1s.at[a, f, k - 1],
                a1r.at[a, f, k - 1],
                dev(z, nxt(y, k), c, x),
            )
            for k in range(1, 4)
        ]

    def gather2(a, f, g1):
        if zfirst(f):
            got[a, f, c, y, z] = own[a, f, j]
            recv(g1)
            return [
                send(
                    got.at[a, f, c, y],
                    got.at[a, f, c, y],
                    a2s.at[a, f, k - 1],
                    a2r.at[a, f, k - 1],
                    dev(z, nxt(y, k), c, x),
                )
                for k in range(1, 4)
            ]
        relay[a, f // 2, y] = own[a, f]
        recv(g1)
        cps = [
            send(
                relay.at[a, f // 2, :, nxt(z, k) // 2],
                got.at[a, f, c, :, z],
                a2s.at[a, f, k - 1],
                a2r.at[a, f, k - 1],
                dev(nxt(z, k), y, c, x),
            )
            for k in range(1, 4)
        ]
        got[a, f, c, :, z] = relay[a, f // 2, :, j]
        return cps

    def gather3(a, f, g2):
        recv(g2)
        return send(
            got.at[a, f, c], got.at[a, f, c], acs.at[a, f], acr.at[a, f], dev(z, y, oc, x)
        )

    def rows_ready(a, f, g3):
        g3.wait_recv()

        def pair(i, _):
            cc, yy, zz = i // 8, (i // 2) % 4, (i % 2) * 2
            two = got[a, f, cc, yy, pl.ds(zz, 2)].astype(F32).reshape(16, F)
            rowmat[a, pl.ds(pl.multiple_of(i * 16, 16), 16), f * F : f * F + F] = two.astype(BF16)
            return 0

        lax.fori_loop(0, 16, pair, 0)

    def partial(a, f):
        left = (act if a == 0 else gpre)[...]
        for t in range(F // TILE):
            lo = f * F + t * TILE
            if a == 0:
                prod = dot(left, down[:, lo : lo + TILE], 1, 0)
            else:
                prod = dot(left, up[lo : lo + TILE, :], 1, 1)
            part[a, f, :, :, :, :, t * TILE : t * TILE + TILE] = prod.reshape(
                2, 4, 4, MOST, TILE
            ).astype(BF16)
        return send(part.at[a, f, oc], swap.at[a, f], bcs.at[a, f], bcr.at[a, f], dev(z, y, oc, x))

    def return1(a, f, cp):
        cp.wait_recv()

        def add(i, _):
            yy, zz = i // 4, i % 4
            swap[a, f, yy, zz] = (
                swap[a, f, yy, zz].astype(F32) + part[a, f, c, yy, zz].astype(F32)
            ).astype(BF16)
            return 0

        lax.fori_loop(0, 16, add, 0)
        if zfirst(f):
            return [
                send(
                    swap.at[a, f, nxt(y, k)],
                    first.at[a, f, k - 1],
                    b1s.at[a, f, k - 1],
                    b1r.at[a, f, k - 1],
                    dev(z, nxt(y, k), c, x),
                )
                for k in range(1, 4)
            ]
        return [
            send(
                swap.at[a, f, :, nxt(z, k)],
                first.at[a, f, k - 1],
                b1s.at[a, f, k - 1],
                b1r.at[a, f, k - 1],
                dev(nxt(z, k), y, c, x),
            )
            for k in range(1, 4)
        ]

    def return2(a, f, cps):
        recv(cps)
        if zfirst(f):

            def add(i, _):
                mid[a, f, i] = (
                    swap[a, f, y, i].astype(F32)
                    + first[a, f, 0, i].astype(F32)
                    + first[a, f, 1, i].astype(F32)
                    + first[a, f, 2, i].astype(F32)
                ).astype(BF16)
                return 0

            lax.fori_loop(0, 4, add, 0)
            return [
                send(
                    mid.at[a, f, nxt(z, k)],
                    second.at[a, f, k - 1, 0],
                    b2s.at[a, f, k - 1],
                    b2r.at[a, f, k - 1],
                    dev(nxt(z, k), y, c, x),
                )
                for k in range(1, 4)
            ]

        def add(i, _):
            mid[a, f, 2 * i + j] = (
                swap[a, f, i, z].astype(F32) + first[a, f, mate, i].astype(F32)
            ).astype(BF16)
            mid[a, f, 2 * i + jo] = (
                first[a, f, 1, i].astype(F32) + first[a, f, 2 - mate, i].astype(F32)
            ).astype(BF16)
            return 0

        lax.fori_loop(0, 4, add, 0)
        return [
            send(
                mid.at[a, f, pl.ds(2 * nxt(y, k), 2)],
                second.at[a, f, k - 1],
                b2s.at[a, f, k - 1],
                b2r.at[a, f, k - 1],
                dev(z, nxt(y, k), c, x),
            )
            for k in range(1, 4)
        ]

    def return3(a, f, cps):
        recv(cps)
        if zfirst(f):
            fin[j] = mid[a, f, z].astype(F32) + second[a, f, mate, 0].astype(F32)
            fin[jo] = second[a, f, 1, 0].astype(F32) + second[a, f, 2 - mate, 0].astype(F32)
        else:
            fin[...] = (
                mid[a, f, pl.ds(2 * y, 2)].astype(F32)
                + second[a, f, 0].astype(F32)
                + second[a, f, 1].astype(F32)
                + second[a, f, 2].astype(F32)
            )
        return fin[...].reshape(2 * MOST, F)

    def to_x(a, f, rows):
        slots[a, f, x] = rows.reshape(2, MOST, F).astype(BF16)
        return [
            send(
                slots.at[a, f, x],
                slots.at[a, f, x],
                xs.at[a, f, k - 1],
                xr.at[a, f, k - 1],
                (me, nxt(x, k)),
            )
            for k in range(1, 4)
        ]

    units = [(a, f) for a in range(2) for f in range(NF)]
    g1 = {u: gather1(*u) for u in units}
    g2, g3 = {}, {}
    for u in units:
        g2[u] = gather2(*u, g1[u])

    recv(tabc)
    tab64 = tables[...].astype(F32).reshape(64, TOK).T.astype(BF16)
    for q in range(4):
        sl = slice(16 * q, 16 * q + 16)
        t16 = dot(tables[q], tok[...], 1, 0)
        c16 = t16 - jnp.mean(t16, axis=1, keepdims=True)
        i16 = lax.rsqrt(jnp.mean(c16 * c16, axis=1, keepdims=True) + 1e-06)
        n64[sl, :] = c16 * i16
        og64[sl, :] = dot(tables[q], og[...], 1, 0).astype(BF16)

    for f in range(NF):
        g3[0, f] = gather3(0, f, g2[0, f])
    in_up.wait()
    for f in range(NF):
        rows_ready(0, f, g3[0, f])
        acc = dot(rowmat[0, :, f * F : f * F + F], up[f * F : f * F + F, :], 1, 0)
        pre[...] = acc if f == 0 else pre[...] + acc
    prev = pre[...]
    tang = jnp.tanh(GELU_C * (prev + 0.044715 * prev * prev * prev))
    act[...] = (0.5 * prev * (1.0 + tang)).astype(BF16)
    pre[...] = 0.5 * (1.0 + tang) + 0.5 * prev * (1.0 - tang * tang) * GELU_C * (
        1.0 + 3.0 * 0.044715 * prev * prev
    )
    outs = [local(rowmat.at[0], rows_hbm, loc.at[4]), local(act, act_hbm, loc.at[5])]
    in_down.wait()
    r0, r1, r2, r3 = {}, {}, {}, {}
    for f in range(NF):
        r0[0, f] = partial(0, f)
    for f in range(NF):
        g3[1, f] = gather3(1, f, g2[1, f])
    for f in range(NF):
        r1[0, f] = return1(0, f, r0[0, f])
    for f in range(NF):
        rows_ready(1, f, g3[1, f])
        acc = dot(rowmat[1, :, f * F : f * F + F], down[:, f * F : f * F + F], 1, 1)
        gact[...] = acc if f == 0 else gact[...] + acc
    gpre[...] = (gact[...] * pre[...]).astype(BF16)
    outs += [local(rowmat.at[1], grads_hbm, loc.at[6]), local(gpre, gp_hbm, loc.at[7])]
    for f in range(NF):
        r0[1, f] = partial(1, f)
    for f in range(NF):
        r2[0, f] = return2(0, f, r1[0, f])
    for f in range(NF):
        r1[1, f] = return1(1, f, r0[1, f])
    grad_w = jnp.zeros((2 * MOST, 1), F32)
    for f in range(NF):
        rows = return3(0, f, r2[0, f])
        grad_w = grad_w + jnp.sum(rows * mix[:, f * F : f * F + F], axis=1, keepdims=True)
        r3[0, f] = to_x(0, f, rows * weight)
    grad_logit = grad_w * weight * (1.0 - weight)
    for f in range(NF):
        r2[1, f] = return2(1, f, r1[1, f])
    row8 = lax.broadcasted_iota(jnp.int32, (8, F), 0)
    for f in range(NF):
        cols = slice(f * F, f * F + F)
        recv(r3[0, f])
        outrows = slots[0, f].astype(F32).reshape(64, F)
        gate_sum = jnp.sum(outrows * og64[:, cols].astype(F32), axis=0, keepdims=True)
        hg = hid16[:, cols].astype(F32) * grad_logit
        gvec[:, cols] = jnp.where(
            row8 == 2,
            gate_sum,
            jnp.where(
                row8 == 3,
                jnp.sum(hg[:MOST], axis=0, keepdims=True),
                jnp.where(row8 == 4, jnp.sum(hg[MOST:], axis=0, keepdims=True), 0.0),
            ),
        )
        outb[:, cols] = (
            tok[:, cols].astype(F32) + gate_ref[:, cols] * dot(tab64, outrows.astype(BF16), 1, 0)
        ).astype(BF16)
    outs += [local(outb, block_hbm, loc.at[8])]
    for f in range(NF):
        rows = return3(1, f, r2[1, f])
        add = [
            grad_logit[MOST * jj : MOST * jj + MOST]
            * router_ref[jj : jj + 1, f * F : f * F + F].astype(F32)
            for jj in range(2)
        ]
        r3[1, f] = to_x(1, f, rows + jnp.concatenate(add, axis=0))
    m1 = jnp.zeros((64, 1), F32)
    m2 = jnp.zeros((64, 1), F32)
    for f in range(NF):
        cols = slice(f * F, f * F + F)
        recv(r3[1, f])
        gh = slots[1, f].astype(F32).reshape(64, F)
        ghn = gh * n64[:, cols]
        gvec[:, cols] = jnp.where(
            row8 == 0,
            jnp.sum(gh, axis=0, keepdims=True),
            jnp.where(row8 == 1, jnp.sum(ghn, axis=0, keepdims=True), gvec[:, cols]),
        )
        one = 1.0 + scale_ref[:, cols]
        g64[:, cols] = gh * one
        m1 = m1 + jnp.sum(gh * one, axis=1, keepdims=True)
        m2 = m2 + jnp.sum(ghn * one, axis=1, keepdims=True)
    for d in range(32):
        vparts[d] = gvec[:, d * 128 : d * 128 + 128]
    v1 = []
    for k in range(1, 32):
        to = (me + k) % 32
        v1.append(send(vparts.at[to], vin.at[me], v1s.at[k - 1], v1r.at[k - 1], (to, x)))
    vin[me] = vparts[me]
    m1 = m1 * (1.0 / D)
    m2 = m2 * (1.0 / D)
    for q in range(4):
        sl = slice(16 * q, 16 * q + 16)
        t16 = dot(tables[q], tok[...], 1, 0)
        c16 = t16 - jnp.mean(t16, axis=1, keepdims=True)
        i16 = lax.rsqrt(jnp.mean(c16 * c16, axis=1, keepdims=True) + 1e-06)
        c64[sl, :] = (i16 * (g64[sl, :] - m1[sl] - n64[sl, :] * m2[sl])).astype(BF16)
    for t in range(D // TILE):
        cols = slice(t * TILE, t * TILE + TILE)
        outt[:, cols] = (og[:, cols].astype(F32) + dot(tab64, c64[:, cols], 1, 0)).astype(BF16)
    outs += [local(outt, tgrad_hbm, loc.at[9])]
    recv(v1)
    total = vin[0]
    for d in range(1, 32):
        total = total + vin[d]
    vsum[me] = total
    v2 = []
    for k in range(1, 32):
        to = (me + k) % 32
        v2.append(send(vsum.at[me], vsum.at[me], v2s.at[k - 1], v2r.at[k - 1], (to, x)))
    recv(v2)
    for d in range(32):
        vec_ref[:, d * 128 : d * 128 + 128] = vsum[d]
    for cp in outs:
        cp.wait()
    for cp in pending:
        cp.wait_send()


def weight_grads_kernel(rows_ref, grads_ref, act_ref, gp_ref, up_ref, down_ref):
    up_ref[0] = dot(rows_ref[...], gp_ref[...], 0, 0).astype(BF16)
    down_ref[0] = dot(act_ref[...], grads_ref[...], 0, 0).astype(BF16)


def per_device(tokens, shift, scale, gate, router, up, down, picks, out_grad):
    hbm = pl.BlockSpec(memory_space=pl.ANY)
    vmem = pl.BlockSpec(memory_space=pltpu.VMEM)
    dma = pltpu.SemaphoreType.DMA
    shape = jax.ShapeDtypeStruct
    block, tgrad, rows, grads, act, gp, vec = pl.pallas_call(
        exchange_kernel,
        out_shape=(
            shape((TOK, D), BF16),
            shape((TOK, D), BF16),
            shape((SLOTS, D), BF16),
            shape((SLOTS, D), BF16),
            shape((SLOTS, HU), BF16),
            shape((SLOTS, HU), BF16),
            shape((8, D), F32),
        ),
        in_specs=[hbm, hbm, vmem, vmem, vmem, vmem, hbm, hbm, vmem],
        out_specs=(hbm, hbm, hbm, hbm, hbm, hbm, vmem),
        scratch_shapes=[
            pltpu.VMEM((TOK, D), BF16),
            pltpu.VMEM((TOK, D), BF16),
            pltpu.VMEM((D, HU), BF16),
            pltpu.VMEM((HU, D), BF16),
            pltpu.VMEM((2, NF, 2, MOST, F), BF16),
            pltpu.VMEM((2, NF, 2, 4, 4, MOST, F), BF16),
            pltpu.VMEM((2, NF // 2, 4, 2, MOST, F), BF16),
            pltpu.VMEM((2, SLOTS, D), BF16),
            pltpu.VMEM((SLOTS, HU), F32),
            pltpu.VMEM((SLOTS, HU), F32),
            pltpu.VMEM((SLOTS, HU), BF16),
            pltpu.VMEM((SLOTS, HU), BF16),
            pltpu.VMEM((2, NF, 2, 4, 4, MOST, F), BF16),
            pltpu.VMEM((2, NF, 4, 4, MOST, F), BF16),
            pltpu.VMEM((2, NF, 3, 4, MOST, F), BF16),
            pltpu.VMEM((2, NF, 8, MOST, F), BF16),
            pltpu.VMEM((2, NF, 3, 2, MOST, F), BF16),
            pltpu.VMEM((2, MOST, F), F32),
            pltpu.VMEM((2, NF, 4, 2, MOST, F), BF16),
            pltpu.VMEM((4, 2 * MOST, TOK), BF16),
            pltpu.VMEM((2 * MOST, D), F32),
            pltpu.VMEM((2 * MOST, D), BF16),
            pltpu.VMEM((64, D), F32),
            pltpu.VMEM((64, D), BF16),
            pltpu.VMEM((64, D), F32),
            pltpu.VMEM((64, D), BF16),
            pltpu.VMEM((TOK, D), BF16),
            pltpu.VMEM((TOK, D), BF16),
            pltpu.VMEM((32, 8, 128), F32),
            pltpu.VMEM((32, 8, 128), F32),
            pltpu.VMEM((32, 8, 128), F32),
            pltpu.VMEM((8, D), F32),
            dma((10,)),
            dma((3,)),
            dma((3,)),
            dma((2, NF, 3)),
            dma((2, NF, 3)),
            dma((2, NF, 3)),
            dma((2, NF, 3)),
            dma((2, NF)),
            dma((2, NF)),
            dma((2, NF)),
            dma((2, NF)),
            dma((2, NF, 3)),
            dma((2, NF, 3)),
            dma((2, NF, 3)),
            dma((2, NF, 3)),
            dma((2, NF, 3)),
            dma((2, NF, 3)),
            dma((31,)),
            dma((31,)),
            dma((31,)),
            dma((31,)),
        ],
        compiler_params=pltpu.CompilerParams(
            collective_id=0, has_side_effects=True, vmem_limit_bytes=56 * 2**20
        ),
        cost_estimate=pl.CostEstimate(
            flops=12 * SLOTS * D * HU, bytes_accessed=24 * 2**20, transcendentals=SLOTS * HU
        ),
    )(
        tokens,
        out_grad,
        shift.reshape(1, D),
        scale.reshape(1, D),
        gate.reshape(1, D),
        router[0].T,
        up,
        down,
        picks[0],
    )
    steps = D // TILE
    full = pl.BlockSpec((SLOTS, HU), lambda i: (0, 0))
    cut = pl.BlockSpec((SLOTS, TILE), lambda i: (0, i))
    up_grad, down_grad = pl.pallas_call(
        weight_grads_kernel,
        grid=(steps,),
        out_shape=(shape((1, D, HU), BF16), shape((1, HU, D), BF16)),
        in_specs=[cut, cut, full, full],
        out_specs=(
            pl.BlockSpec((1, TILE, HU), lambda i: (0, i, 0)),
            pl.BlockSpec((1, HU, TILE), lambda i: (0, 0, i)),
        ),
        cost_estimate=pl.CostEstimate(
            flops=4 * SLOTS * D * HU, bytes_accessed=13 * 2**20, transcendentals=0
        ),
    )(rows, grads, act, gp)
    return (
        block,
        tgrad,
        up_grad,
        down_grad,
        vec[3:5].T[None],
        vec[0],
        vec[1],
        vec[2],
    )


def solution(mesh):
    in_specs = (
        P("ctx", None),
        P(),
        P(),
        P(),
        P("exp", None, None),
        P("exp", None, "ctx"),
        P("exp", "ctx", None),
        P("exp", None, None),
        P("ctx", None),
    )
    out_specs = (
        P("ctx", None),
        P("ctx", None),
        P("exp", None, "ctx"),
        P("exp", "ctx", None),
        P("exp", None, None),
        P(),
        P(),
        P(),
    )
    return jax.shard_map(
        per_device, mesh=mesh, in_specs=in_specs, out_specs=out_specs, check_vma=False
    )
```

time: 532 us -> 89.9 us (0.17)
  waiting for transfers between devices: 454 us -> 0 us
  Pallas kernels: 0 us -> 83.6 us
  matrix products: 35.8 us -> 0 us
  other arithmetic: 21.9 us -> 0 us
  between operations: 14.3 us -> 0.66 us
    psum x2 -> x0, waiting for transfers between devices: 181 us -> none  [the longest x1 93 us: per_device(): router_total, vector_total = lax.psum((router_part, vectors), 'ctx')]
    reduce_scatter x2 -> x0, waiting for transfers between devices: 176 us -> none  [send_back(): lax.psum_scatter((product_rows * group_mask).reshape(pair_count * MOST *...]
    all_gather x2 -> x0, waiting for transfers between devices: 97.9 us -> none  [deliver(): everyone = lax.all_gather(row_data, 'ctx', axis=0, tiled=True)]
    pallas_call x0 -> x2, Pallas kernels: none -> 83.6 us  [the longest x1 75 us: per_device(): pl.pallas_call(exchange_kernel, out_shape=(shape((TOK, D), BF16), shape((...]
    dot_general x17 -> x0, matrix products: 35.8 us -> none  [the longest x1 5.15 us: per_device(): lax.dot_general(activated, expert_grads, (((0,), (0,)), ((), ())), prefer...]
    mul x3 -> x0, other arithmetic: 8.97 us -> none  [the longest x2 8.97 us: send_back(): product_rows * group_mask]
    reduce_sum x4 -> x0, other arithmetic: 8.94 us -> none  [the longest x1 4.34 us: per_device(): jnp.sum(grad_in * mixture, axis=0)]
  transfers between devices with their start and end apart: 6 -> 0, of which waited for: 6 -> 0; matrix products, arithmetic and copies ran while one was open for 3% -> 0% of each run, Pallas kernels for 0% -> 0%
where the time goes in v1:
time: 89.9 us; the launch traced here: 89.5 us
  Pallas kernels  83.6 us (93%)
  local copies, waits for them, and re-layouts  5.27 us (6%)
    pallas_call x1, Pallas kernels, per_device(): pl.pallas_call(exchange_kernel, out_shape=(shape((TOK, D), BF16), shape((...  75 us
    pallas_call x1, Pallas kernels, per_device(): pl.pallas_call(weight_grads_kernel, grid=(steps,), out_shape=(shape((1, D...  8.55 us
    unnamed x6, local copies, waits for them, and re-layouts  1.95 us

profile of v1, /device:TPU:1, one launch (start us, length us, event | category | flops | bytes accessed | tf_op | source)
XLA Modules:
  0.0 89.5 jit_solution(11075994189373621031)
XLA Ops:
  0.6 75.0 %shard_map.152 = (bf16[128,4096]{1,0:T(8,128)(2,1)}, bf16[128,4096]{1,0:T(8,128)(2,1)}, bf16[256,4096]{1,0:T(8,128)(2,1)}, bf16[256,4096]{1,0:T(8,128)(2,1)}, bf...) custom-call(bf16[128,4096]{1,0:T(8,128)(2,1)} %tok_hbm.1, bf16[128,4096]{1,0:T(8,128)(2,1)} %og_hbm.1, ...), custom_call_target="tpu_custom_call" | custom-call | flops 6442450944 | bytes 25165824 | tf_op jit(solution)/shard_map/pallas_call | solution.py:535
  75.7 0.0 copy-start.1
  75.7 1.6 %slice_bitcast_fusion = f32[1,4096,2]{1,2,0:T(2,128)} fusion(f32[8,4096]{1,0:T(8,128)} %get-tuple-element.25), kind=kLoop, calls=%fused_computation | loop fusion | bytes 65536 | tf_op jit(solution)/shard_map/broadcast_in_dim | solution.py:641
  77.3 1.7 %fusion = (f32[1,4096]{1,0:T(1,128)}, f32[1,4096]{1,0:T(1,128)}, f32[1,4096]{1,0:T(1,128)}) fusion(f32[8,4096]{1,0:T(8,128)} %get-tuple-element.25), kind=kLoop, calls=%fused_computation.1 | loop fusion | bytes 98304 | tf_op jit(solution)/shard_map/slice | solution.py:644
  79.0 0.0 copy-start
  79.0 8.5 %shard_map.153 = (bf16[1,4096,512]{2,1,0:T(8,128)(2,1)}, bf16[1,512,4096]{2,1,0:T(8,128)(2,1)}) custom-call(bf16[256,4096]{1,0:T(8,128)(2,1)} %get-tuple-element.19.rows_ref, bf16[256,4096]{1,0:T(8,128)(2,1)} %get-tuple-element.20.grads_ref, bf16[256,512]{1,0:T(8,128)(2,1)} %get-tuple-element.21.act_ref, bf16[256,512]{1,0:T(8,128)(2,1)} %get-tuple-element.22.gp_ref), custom_call_target="tpu_custom_call" | custom-call | flops 2147483648 | bytes 13631488 | tf_op jit(solution)/shard_map/pallas_call | solution.py:623
  87.5 0.0 copy-done.1
  87.5 1.0 %copy.19 = bf16[128,4096]{1,0:T(8,128)(2,1)} copy(bf16[128,4096]{1,0:T(8,128)(2,1)S(1)} %copy-done.1) | data formatting | bytes 2097152
  88.5 0.0 copy-done
  88.5 1.0 %copy.20 = bf16[128,4096]{1,0:T(8,128)(2,1)} copy(bf16[128,4096]{1,0:T(8,128)(2,1)S(1)} %copy-done) | data formatting | bytes 2097152
Async XLA Ops:
  75.7 11.9 %copy-start.1 = (bf16[128,4096]{1,0:T(8,128)(2,1)S(1)}, bf16[128,4096]{1,0:T(8,128)(2,1)}, u32[]{:S(2)}) copy-start(bf16[128,4096]{1,0:T(8,128)(2,1)} %get-tuple-element.37) | copy-start | bytes 3145732
  79.0 9.5 %copy-start = (bf16[128,4096]{1,0:T(8,128)(2,1)S(1)}, bf16[128,4096]{1,0:T(8,128)(2,1)}, u32[]{:S(2)}) copy-start(bf16[128,4096]{1,0:T(8,128)(2,1)} %get-tuple-element.38) | copy-start | bytes 3145732

commit v2 on v1

--- a/solution.py
+++ b/solution.py
@@ -34,12 +34,13 @@
     up_hbm,
     down_hbm,
     picks_ref,
-    block_hbm,
-    tgrad_hbm,
     rows_hbm,
     grads_hbm,
     act_hbm,
     gp_hbm,
+    mixrows_hbm,
+    corr_hbm,
+    table_ref,
     vec_ref,
     tok,
     og,
@@ -67,12 +68,12 @@
     og64,
     g64,
     c64,
-    outb,
-    outt,
-    vparts,
-    vin,
-    vsum,
-    gvec,
+    x64,
+    vsrc,
+    vswap,
+    vy,
+    vz,
+    vfin,
     loc,
     tab_s,
     tab_r,
@@ -90,10 +91,8 @@
     b2r,
     xs,
     xr,
-    v1s,
-    v1r,
-    v2s,
-    v2r,
+    vs,
+    vr,
 ):
     me = lax.axis_index("ctx")
     x = lax.axis_index("exp")
@@ -130,9 +129,10 @@
     in_down = local(down_hbm.at[0], down, loc.at[3])
 
     bar = pltpu.get_barrier_semaphore()
-    for k in range(1, 32):
-        pl.semaphore_signal(bar, inc=1, device_id=((me + k) % 32, x), device_id_type=MESH)
+    pl.semaphore_signal(bar, inc=1, device_id=dev(z, y, oc, x), device_id_type=MESH)
     for k in range(1, 4):
+        pl.semaphore_signal(bar, inc=1, device_id=dev(nxt(z, k), y, c, x), device_id_type=MESH)
+        pl.semaphore_signal(bar, inc=1, device_id=dev(z, nxt(y, k), c, x), device_id_type=MESH)
         pl.semaphore_signal(bar, inc=1, device_id=(me, nxt(x, k)), device_id_type=MESH)
 
     lanes = lax.broadcasted_iota(jnp.int32, (MOST, TOK), 1)
@@ -181,7 +181,7 @@
         for jj in range(2):
             own[1, f, jj] = gradv[MOST * jj : MOST * jj + MOST, f * F : f * F + F].astype(BF16)
 
-    pl.semaphore_wait(bar, 34)
+    pl.semaphore_wait(bar, 10)
 
     tabc = [
         send(tables.at[x], tables.at[x], tab_s.at[k - 1], tab_r.at[k - 1], (me, nxt(x, k)))
@@ -383,26 +383,90 @@
             for k in range(1, 4)
         ]
 
-    units = [(a, f) for a in range(2) for f in range(NF)]
-    g1 = {u: gather1(*u) for u in units}
-    g2, g3 = {}, {}
-    for u in units:
-        g2[u] = gather2(*u, g1[u])
+    def spread(row, stage, cc, n):
+        for i in range(D // TILE):
+            vsrc[stage, cc, n, i : i + 1, :] = row[:, i * TILE : i * TILE + TILE]
+
+    def vsum1(s, n):
+        return send(
+            vsrc.at[s, oc, pl.ds(0, n)],
+            vswap.at[s, pl.ds(0, n)],
+            vs.at[s, 0],
+            vr.at[s, 0],
+            dev(z, y, oc, x),
+        )
+
+    def vsum2(s, n, cp):
+        cp.wait_recv()
+        vy[s, y, pl.ds(0, n)] = vsrc[s, c, pl.ds(0, n)] + vswap[s, pl.ds(0, n)]
+        return [
+            send(
+                vy.at[s, y, pl.ds(0, n)],
+                vy.at[s, y, pl.ds(0, n)],
+                vs.at[s, k],
+                vr.at[s, k],
+                dev(z, nxt(y, k), c, x),
+            )
+            for k in range(1, 4)
+        ]
+
+    def vsum3(s, n, cps):
+        recv(cps)
+        cut = pl.ds(0, n)
+        vz[s, z, cut] = (vy[s, 0, cut] + vy[s, 1, cut]) + (vy[s, 2, cut] + vy[s, 3, cut])
+        return [
+            send(
+                vz.at[s, z, cut],
+                vz.at[s, z, cut],
+                vs.at[s, 3 + k],
+                vr.at[s, 3 + k],
+                dev(nxt(z, k), y, c, x),
+            )
+            for k in range(1, 4)
+        ]
+
+    def vsum4(s, n, cps):
+        recv(cps)
+        cut = pl.ds(0, n)
+        vfin[s, c, cut] = (vz[s, 0, cut] + vz[s, 1, cut]) + (vz[s, 2, cut] + vz[s, 3, cut])
+        return send(
+            vfin.at[s, c, cut], vfin.at[s, c, cut], vs.at[s, 7], vr.at[s, 7], dev(z, y, oc, x)
+        )
+
+    drained = [0]
+
+    def drain():
+        for cp in pending[drained[0] :]:
+            cp.wait_send()
+        drained[0] = len(pending)
+
+    parts = range(NF)
+    g1, g2, g3 = {}, {}, {}
+    for f in parts:
+        g1[0, f] = gather1(0, f)
+    for f in parts:
+        g2[0, f] = gather2(0, f, g1[0, f])
+    for f in parts:
+        g1[1, f] = gather1(1, f)
 
     recv(tabc)
-    tab64 = tables[...].astype(F32).reshape(64, TOK).T.astype(BF16)
+    tabt = tables[...].astype(F32).reshape(64, TOK).T.astype(BF16)
+    table_ref[...] = tabt
+    invs = []
     for q in range(4):
         sl = slice(16 * q, 16 * q + 16)
         t16 = dot(tables[q], tok[...], 1, 0)
         c16 = t16 - jnp.mean(t16, axis=1, keepdims=True)
         i16 = lax.rsqrt(jnp.mean(c16 * c16, axis=1, keepdims=True) + 1e-06)
+        invs.append(i16)
         n64[sl, :] = c16 * i16
         og64[sl, :] = dot(tables[q], og[...], 1, 0).astype(BF16)
 
-    for f in range(NF):
+    for f in parts:
         g3[0, f] = gather3(0, f, g2[0, f])
+        g2[1, f] = gather2(1, f, g1[1, f])
     in_up.wait()
-    for f in range(NF):
+    for f in parts:
         rows_ready(0, f, g3[0, f])
         acc = dot(rowmat[0, :, f * F : f * F + F], up[f * F : f * F + F, :], 1, 0)
         pre[...] = acc if f == 0 else pre[...] + acc
@@ -415,53 +479,48 @@
     outs = [local(rowmat.at[0], rows_hbm, loc.at[4]), local(act, act_hbm, loc.at[5])]
     in_down.wait()
     r0, r1, r2, r3 = {}, {}, {}, {}
-    for f in range(NF):
+    for f in parts:
         r0[0, f] = partial(0, f)
-    for f in range(NF):
+    for f in parts:
         g3[1, f] = gather3(1, f, g2[1, f])
-    for f in range(NF):
+    for f in parts:
         r1[0, f] = return1(0, f, r0[0, f])
-    for f in range(NF):
+    for f in parts:
         rows_ready(1, f, g3[1, f])
         acc = dot(rowmat[1, :, f * F : f * F + F], down[:, f * F : f * F + F], 1, 1)
         gact[...] = acc if f == 0 else gact[...] + acc
     gpre[...] = (gact[...] * pre[...]).astype(BF16)
     outs += [local(rowmat.at[1], grads_hbm, loc.at[6]), local(gpre, gp_hbm, loc.at[7])]
-    for f in range(NF):
+    for f in parts:
         r0[1, f] = partial(1, f)
-    for f in range(NF):
+    for f in parts:
         r2[0, f] = return2(0, f, r1[0, f])
-    for f in range(NF):
+    for f in parts:
         r1[1, f] = return1(1, f, r0[1, f])
     grad_w = jnp.zeros((2 * MOST, 1), F32)
-    for f in range(NF):
+    for f in parts:
         rows = return3(0, f, r2[0, f])
         grad_w = grad_w + jnp.sum(rows * mix[:, f * F : f * F + F], axis=1, keepdims=True)
         r3[0, f] = to_x(0, f, rows * weight)
     grad_logit = grad_w * weight * (1.0 - weight)
-    for f in range(NF):
+    for f in parts:
         r2[1, f] = return2(1, f, r1[1, f])
-    row8 = lax.broadcasted_iota(jnp.int32, (8, F), 0)
-    for f in range(NF):
+    hg = hid16[...].astype(F32) * grad_logit
+    spread(jnp.sum(hg[:MOST], axis=0, keepdims=True), 0, 0, 1)
+    spread(jnp.sum(hg[MOST:], axis=0, keepdims=True), 0, 1, 0)
+    vsrc[0, 1, 1] = jnp.zeros((8, TILE), F32)
+    sums = []
+    for f in parts:
         cols = slice(f * F, f * F + F)
         recv(r3[0, f])
         outrows = slots[0, f].astype(F32).reshape(64, F)
-        gate_sum = jnp.sum(outrows * og64[:, cols].astype(F32), axis=0, keepdims=True)
-        hg = hid16[:, cols].astype(F32) * grad_logit
-        gvec[:, cols] = jnp.where(
-            row8 == 2,
-            gate_sum,
-            jnp.where(
-                row8 == 3,
-                jnp.sum(hg[:MOST], axis=0, keepdims=True),
-                jnp.where(row8 == 4, jnp.sum(hg[MOST:], axis=0, keepdims=True), 0.0),
-            ),
-        )
-        outb[:, cols] = (
-            tok[:, cols].astype(F32) + gate_ref[:, cols] * dot(tab64, outrows.astype(BF16), 1, 0)
-        ).astype(BF16)
-    outs += [local(outb, block_hbm, loc.at[8])]
-    for f in range(NF):
+        sums.append(jnp.sum(outrows * og64[:, cols].astype(F32), axis=0, keepdims=True))
+        x64[:, cols] = outrows.astype(BF16)
+    spread(jnp.concatenate(sums, axis=1), 0, 0, 0)
+    va = vsum1(0, 2)
+    outs += [local(x64, mixrows_hbm, loc.at[8])]
+    drain()
+    for f in parts:
         rows = return3(1, f, r2[1, f])
         add = [
             grad_logit[MOST * jj : MOST * jj + MOST]
@@ -469,62 +528,87 @@
             for jj in range(2)
         ]
         r3[1, f] = to_x(1, f, rows + jnp.concatenate(add, axis=0))
+    vb = vsum2(0, 2, va)
     m1 = jnp.zeros((64, 1), F32)
     m2 = jnp.zeros((64, 1), F32)
-    for f in range(NF):
+    sums, sums_n = [], []
+    for f in parts:
         cols = slice(f * F, f * F + F)
         recv(r3[1, f])
         gh = slots[1, f].astype(F32).reshape(64, F)
         ghn = gh * n64[:, cols]
-        gvec[:, cols] = jnp.where(
-            row8 == 0,
-            jnp.sum(gh, axis=0, keepdims=True),
-            jnp.where(row8 == 1, jnp.sum(ghn, axis=0, keepdims=True), gvec[:, cols]),
-        )
+        sums.append(jnp.sum(gh, axis=0, keepdims=True))
+        sums_n.append(jnp.sum(ghn, axis=0, keepdims=True))
         one = 1.0 + scale_ref[:, cols]
         g64[:, cols] = gh * one
         m1 = m1 + jnp.sum(gh * one, axis=1, keepdims=True)
         m2 = m2 + jnp.sum(ghn * one, axis=1, keepdims=True)
-    for d in range(32):
-        vparts[d] = gvec[:, d * 128 : d * 128 + 128]
-    v1 = []
-    for k in range(1, 32):
-        to = (me + k) % 32
-        v1.append(send(vparts.at[to], vin.at[me], v1s.at[k - 1], v1r.at[k - 1], (to, x)))
-    vin[me] = vparts[me]
+    spread(jnp.concatenate(sums, axis=1), 1, 0, 0)
+    spread(jnp.concatenate(sums_n, axis=1), 1, 1, 0)
+    wa = vsum1(1, 1)
+    vc = vsum3(0, 2, vb)
+    wb = vsum2(1, 1, wa)
     m1 = m1 * (1.0 / D)
     m2 = m2 * (1.0 / D)
     for q in range(4):
         sl = slice(16 * q, 16 * q + 16)
-        t16 = dot(tables[q], tok[...], 1, 0)
-        c16 = t16 - jnp.mean(t16, axis=1, keepdims=True)
-        i16 = lax.rsqrt(jnp.mean(c16 * c16, axis=1, keepdims=True) + 1e-06)
-        c64[sl, :] = (i16 * (g64[sl, :] - m1[sl] - n64[sl, :] * m2[sl])).astype(BF16)
-    for t in range(D // TILE):
-        cols = slice(t * TILE, t * TILE + TILE)
-        outt[:, cols] = (og[:, cols].astype(F32) + dot(tab64, c64[:, cols], 1, 0)).astype(BF16)
-    outs += [local(outt, tgrad_hbm, loc.at[9])]
-    recv(v1)
-    total = vin[0]
-    for d in range(1, 32):
-        total = total + vin[d]
-    vsum[me] = total
-    v2 = []
-    for k in range(1, 32):
-        to = (me + k) % 32
-        v2.append(send(vsum.at[me], vsum.at[me], v2s.at[k - 1], v2r.at[k - 1], (to, x)))
-    recv(v2)
-    for d in range(32):
-        vec_ref[:, d * 128 : d * 128 + 128] = vsum[d]
+        c64[sl, :] = (invs[q] * (g64[sl, :] - m1[sl] - n64[sl, :] * m2[sl])).astype(BF16)
+    outs += [local(c64, corr_hbm, loc.at[9])]
+    vd = vsum4(0, 2, vc)
+    wc = vsum3(1, 1, wb)
+    drain()
+    vd.wait_recv()
+    vec_ref[2] = vfin[0, 0, 0]
+    vec_ref[3] = vfin[0, 0, 1]
+    vec_ref[4] = vfin[0, 1, 0]
+    wd = vsum4(1, 1, wc)
     for cp in outs:
         cp.wait()
-    for cp in pending:
-        cp.wait_send()
-
-
-def weight_grads_kernel(rows_ref, grads_ref, act_ref, gp_ref, up_ref, down_ref):
+    wd.wait_recv()
+    vec_ref[0] = vfin[1, 0, 0]
+    vec_ref[1] = vfin[1, 1, 0]
+    drain()
+
+
+def finish_kernel(
+    rows_ref,
+    grads_ref,
+    act_ref,
+    gp_ref,
+    tok_ref,
+    og_ref,
+    gate_ref,
+    table_ref,
+    mixrows_ref,
+    corr_ref,
+    vec_ref,
+    up_ref,
+    down_ref,
+    block_ref,
+    tgrad_ref,
+    shift_ref,
+    scale_ref,
+    ggrad_ref,
+    router_ref,
+):
     up_ref[0] = dot(rows_ref[...], gp_ref[...], 0, 0).astype(BF16)
     down_ref[0] = dot(act_ref[...], grads_ref[...], 0, 0).astype(BF16)
+    block_ref[...] = (
+        tok_ref[...].astype(F32) + gate_ref[...] * dot(table_ref[...], mixrows_ref[...], 1, 0)
+    ).astype(BF16)
+    tgrad_ref[...] = (
+        og_ref[...].astype(F32) + dot(table_ref[...], corr_ref[...], 1, 0)
+    ).astype(BF16)
+
+    @pl.when(pl.program_id(0) == 0)
+    def _():
+        for i in range(D // TILE):
+            cols = slice(i * TILE, i * TILE + TILE)
+            shift_ref[:, cols] = vec_ref[0, i : i + 1, :]
+            scale_ref[:, cols] = vec_ref[1, i : i + 1, :]
+            ggrad_ref[:, cols] = vec_ref[2, i : i + 1, :]
+            router_ref[0:1, cols] = vec_ref[3, i : i + 1, :]
+            router_ref[1:2, cols] = vec_ref[4, i : i + 1, :]
 
 
 def per_device(tokens, shift, scale, gate, router, up, down, picks, out_grad):
@@ -532,19 +616,20 @@
     vmem = pl.BlockSpec(memory_space=pltpu.VMEM)
     dma = pltpu.SemaphoreType.DMA
     shape = jax.ShapeDtypeStruct
-    block, tgrad, rows, grads, act, gp, vec = pl.pallas_call(
+    rows, grads, act, gp, mixrows, corr, table, vec = pl.pallas_call(
         exchange_kernel,
         out_shape=(
-            shape((TOK, D), BF16),
-            shape((TOK, D), BF16),
             shape((SLOTS, D), BF16),
             shape((SLOTS, D), BF16),
             shape((SLOTS, HU), BF16),
             shape((SLOTS, HU), BF16),
-            shape((8, D), F32),
+            shape((64, D), BF16),
+            shape((64, D), BF16),
+            shape((TOK, 64), BF16),
+            shape((5, 8, TILE), F32),
         ),
         in_specs=[hbm, hbm, vmem, vmem, vmem, vmem, hbm, hbm, vmem],
-        out_specs=(hbm, hbm, hbm, hbm, hbm, hbm, vmem),
+        out_specs=(hbm, hbm, hbm, hbm, hbm, hbm, vmem, vmem),
         scratch_shapes=[
             pltpu.VMEM((TOK, D), BF16),
             pltpu.VMEM((TOK, D), BF16),
@@ -572,12 +657,12 @@
             pltpu.VMEM((64, D), BF16),
             pltpu.VMEM((64, D), F32),
             pltpu.VMEM((64, D), BF16),
-            pltpu.VMEM((TOK, D), BF16),
-            pltpu.VMEM((TOK, D), BF16),
-            pltpu.VMEM((32, 8, 128), F32),
-            pltpu.VMEM((32, 8, 128), F32),
-            pltpu.VMEM((32, 8, 128), F32),
-            pltpu.VMEM((8, D), F32),
+            pltpu.VMEM((64, D), BF16),
+            pltpu.VMEM((2, 2, 2, 8, TILE), F32),
+            pltpu.VMEM((2, 2, 8, TILE), F32),
+            pltpu.VMEM((2, 4, 2, 8, TILE), F32),
+            pltpu.VMEM((2, 4, 2, 8, TILE), F32),
+            pltpu.VMEM((2, 2, 2, 8, TILE), F32),
             dma((10,)),
             dma((3,)),
             dma((3,)),
@@ -595,10 +680,8 @@
             dma((2, NF, 3)),
             dma((2, NF, 3)),
             dma((2, NF, 3)),
-            dma((31,)),
-            dma((31,)),
-            dma((31,)),
-            dma((31,)),
+            dma((2, 8)),
+            dma((2, 8)),
         ],
         compiler_params=pltpu.CompilerParams(
             collective_id=0, has_side_effects=True, vmem_limit_bytes=56 * 2**20
@@ -618,30 +701,58 @@
         picks[0],
     )
     steps = D // TILE
-    full = pl.BlockSpec((SLOTS, HU), lambda i: (0, 0))
-    cut = pl.BlockSpec((SLOTS, TILE), lambda i: (0, i))
-    up_grad, down_grad = pl.pallas_call(
-        weight_grads_kernel,
+    one = lambda i: (0, 0)
+    col = lambda i: (0, i)
+    vecs = pl.BlockSpec((1, D), one)
+    up_grad, down_grad, block, tgrad, shift_g, scale_g, gate_g, router_g = pl.pallas_call(
+        finish_kernel,
         grid=(steps,),
-        out_shape=(shape((1, D, HU), BF16), shape((1, HU, D), BF16)),
-        in_specs=[cut, cut, full, full],
+        out_shape=(
+            shape((1, D, HU), BF16),
+            shape((1, HU, D), BF16),
+            shape((TOK, D), BF16),
+            shape((TOK, D), BF16),
+            shape((1, D), F32),
+            shape((1, D), F32),
+            shape((1, D), F32),
+            shape((2, D), F32),
+        ),
+        in_specs=[
+            pl.BlockSpec((SLOTS, TILE), col),
+            pl.BlockSpec((SLOTS, TILE), col),
+            pl.BlockSpec((SLOTS, HU), one),
+            pl.BlockSpec((SLOTS, HU), one),
+            pl.BlockSpec((TOK, TILE), col),
+            pl.BlockSpec((TOK, TILE), col),
+            pl.BlockSpec((1, TILE), col),
+            pl.BlockSpec((TOK, 64), one),
+            pl.BlockSpec((64, TILE), col),
+            pl.BlockSpec((64, TILE), col),
+            pl.BlockSpec((5, 8, TILE), lambda i: (0, 0, 0)),
+        ],
         out_specs=(
             pl.BlockSpec((1, TILE, HU), lambda i: (0, i, 0)),
             pl.BlockSpec((1, HU, TILE), lambda i: (0, 0, i)),
+            pl.BlockSpec((TOK, TILE), col),
+            pl.BlockSpec((TOK, TILE), col),
+            vecs,
+            vecs,
+            vecs,
+            pl.BlockSpec((2, D), one),
         ),
         cost_estimate=pl.CostEstimate(
-            flops=4 * SLOTS * D * HU, bytes_accessed=13 * 2**20, transcendentals=0
+            flops=4 * SLOTS * D * HU, bytes_accessed=18 * 2**20, transcendentals=0
         ),
-    )(rows, grads, act, gp)
+    )(rows, grads, act, gp, tokens, out_grad, gate.reshape(1, D), table, mixrows, corr, vec)
     return (
         block,
         tgrad,
         up_grad,
         down_grad,
-        vec[3:5].T[None],
-        vec[0],
-        vec[1],
-        vec[2],
+        router_g.T[None],
+        shift_g[0],
+        scale_g[0],
+        gate_g[0],
     )
 
 

time: 89.9 us -> 83 us (0.923)
  local copies, waits for them, and re-layouts: 5.27 us -> 0 us
  Pallas kernels: 83.6 us -> 82 us
    unnamed x6 -> x0, local copies, waits for them, and re-layouts: 1.95 us -> none
    slice x1 -> x0, local copies, waits for them, and re-layouts: 1.7 us -> none  [per_device(): vec[2]]
    broadcast_in_dim x1 -> x0, local copies, waits for them, and re-layouts: 1.62 us -> none  [per_device(): vec[3:5].T[None]]
    pallas_call x2, Pallas kernels: 83.6 us -> 82 us  [the longest x1 70.6 us: per_device(): pl.pallas_call(exchange_kernel, out_shape=(shape((SLOTS, D), BF16), shape...]
where the time goes in v2:
time: 83 us; the launch traced here: 82.6 us
  Pallas kernels  82 us (99%)
    pallas_call x1, Pallas kernels, per_device(): pl.pallas_call(exchange_kernel, out_shape=(shape((SLOTS, D), BF16), shape...  70.6 us
    pallas_call x1, Pallas kernels, per_device(): pl.pallas_call(finish_kernel, grid=(steps,), out_shape=(shape((1, D, HU),...  11.4 us

profile of v2, /device:TPU:1, one launch (start us, length us, event | category | flops | bytes accessed | tf_op | source)
XLA Modules:
  0.0 82.6 jit_solution(5199339262123169138)
XLA Ops:
  0.6 70.6 %shard_map.152 = (bf16[256,4096]{1,0:T(8,128)(2,1)}, bf16[256,4096]{1,0:T(8,128)(2,1)}, bf16[256,512]{1,0:T(8,128)(2,1)}, bf16[256,512]{1,0:T(8,128)(2,1)}, bf16...) custom-call(bf16[128,4096]{1,0:T(8,128)(2,1)} %tok_ref.1, ...), custom_call_target="tpu_custom_call" | custom-call | flops 6442450944 | bytes 25165824 | tf_op jit(solution)/shard_map/pallas_call | solution.py:619
  71.2 11.4 %shard_map.153 = (bf16[1,4096,512]{2,1,0:T(8,128)(2,1)}, bf16[1,512,4096]{2,1,0:T(8,128)(2,1)}, bf16[128,4096]{1,0:T(8,128)(2,1)}, bf16[128,4096]{1,0:T(8,128)(2...) custom-call(bf16[256,4096]{1,0:T(8,128)(2,1)} %get-tuple-element.24.rows_ref, ...), custom_call_target="tpu_custom_call" | custom-call | flops 2147483648 | bytes 18874368 | tf_op jit(solution)/shard_map/pallas_call | solution.py:707

commit v3 on v2

--- a/solution.py
+++ b/solution.py
@@ -14,9 +14,10 @@
 HU = 512
 TOK = 128
 MOST = 8
-NF = 2
+NF = 4
 F = D // NF
 TILE = 512
+STEP = 1024
 SLOTS = 32 * MOST
 
 
@@ -34,26 +35,23 @@
     up_hbm,
     down_hbm,
     picks_ref,
-    rows_hbm,
-    grads_hbm,
-    act_hbm,
-    gp_hbm,
-    mixrows_hbm,
-    corr_hbm,
+    rowmat0,
+    rowmat1,
+    act,
+    gpre,
+    x64,
+    c64,
+    tok,
+    og,
     table_ref,
     vec_ref,
-    tok,
-    og,
     up,
     down,
     own,
     got,
     relay,
-    rowmat,
     pre,
     gact,
-    act,
-    gpre,
     part,
     swap,
     first,
@@ -67,13 +65,12 @@
     n64,
     og64,
     g64,
-    c64,
-    x64,
+    n16,
     vsrc,
-    vswap,
     vy,
+    vx,
+    vw,
     vz,
-    vfin,
     loc,
     tab_s,
     tab_r,
@@ -93,6 +90,8 @@
     xr,
     vs,
     vr,
+    ws,
+    wr,
 ):
     me = lax.axis_index("ctx")
     x = lax.axis_index("exp")
@@ -125,15 +124,16 @@
 
     in_tok = local(tok_hbm, tok, loc.at[0])
     in_og = local(og_hbm, og, loc.at[1])
-    in_up = local(up_hbm.at[0], up, loc.at[2])
-    in_down = local(down_hbm.at[0], down, loc.at[3])
 
     bar = pltpu.get_barrier_semaphore()
     pl.semaphore_signal(bar, inc=1, device_id=dev(z, y, oc, x), device_id_type=MESH)
     for k in range(1, 4):
         pl.semaphore_signal(bar, inc=1, device_id=dev(nxt(z, k), y, c, x), device_id_type=MESH)
         pl.semaphore_signal(bar, inc=1, device_id=dev(z, nxt(y, k), c, x), device_id_type=MESH)
+        pl.semaphore_signal(bar, inc=1, device_id=dev(nxt(z, k), y, oc, x), device_id_type=MESH)
+        pl.semaphore_signal(bar, inc=1, device_id=dev(z, nxt(y, k), oc, x), device_id_type=MESH)
         pl.semaphore_signal(bar, inc=1, device_id=(me, nxt(x, k)), device_id_type=MESH)
+        pl.semaphore_signal(bar, inc=1, device_id=dev(z, y, oc, nxt(x, k)), device_id_type=MESH)
 
     lanes = lax.broadcasted_iota(jnp.int32, (MOST, TOK), 1)
     subl = lax.broadcasted_iota(jnp.int32, (MOST, TOK), 0)
@@ -158,6 +158,7 @@
     cen = trow - jnp.mean(trow, axis=1, keepdims=True)
     inv = lax.rsqrt(jnp.mean(cen * cen, axis=1, keepdims=True) + 1e-06)
     row_there = jnp.sum(table.astype(F32), axis=1, keepdims=True)
+    n16[...] = cen * inv
     hid = ((cen * inv * (1.0 + scale_ref[...]) + shift_ref[...]) * row_there).astype(BF16)
     hid16[...] = hid
     hidf = hid.astype(F32)
@@ -173,15 +174,7 @@
     for f in range(NF):
         for jj in range(2):
             own[0, f, jj] = hidf[MOST * jj : MOST * jj + MOST, f * F : f * F + F].astype(BF16)
-    in_og.wait()
-    mixv = dot(table, og[...], 1, 0) * gate_ref[...]
-    mix[...] = mixv
-    gradv = weight * mixv
-    for f in range(NF):
-        for jj in range(2):
-            own[1, f, jj] = gradv[MOST * jj : MOST * jj + MOST, f * F : f * F + F].astype(BF16)
-
-    pl.semaphore_wait(bar, 10)
+    pl.semaphore_wait(bar, 19)
 
     tabc = [
         send(tables.at[x], tables.at[x], tab_s.at[k - 1], tab_r.at[k - 1], (me, nxt(x, k)))
@@ -259,7 +252,7 @@
         def pair(i, _):
             cc, yy, zz = i // 8, (i // 2) % 4, (i % 2) * 2
             two = got[a, f, cc, yy, pl.ds(zz, 2)].astype(F32).reshape(16, F)
-            rowmat[a, pl.ds(pl.multiple_of(i * 16, 16), 16), f * F : f * F + F] = two.astype(BF16)
+            (rowmat1 if a else rowmat0)[pl.ds(pl.multiple_of(i * 16, 16), 16), f * F : f * F + F] = two.astype(BF16)
             return 0
 
         lax.fori_loop(0, 16, pair, 0)
@@ -388,50 +381,77 @@
             vsrc[stage, cc, n, i : i + 1, :] = row[:, i * TILE : i * TILE + TILE]
 
     def vsum1(s, n):
-        return send(
-            vsrc.at[s, oc, pl.ds(0, n)],
-            vswap.at[s, pl.ds(0, n)],
-            vs.at[s, 0],
-            vr.at[s, 0],
-            dev(z, y, oc, x),
-        )
-
-    def vsum2(s, n, cp):
-        cp.wait_recv()
-        vy[s, y, pl.ds(0, n)] = vsrc[s, c, pl.ds(0, n)] + vswap[s, pl.ds(0, n)]
+        cut = pl.ds(0, n)
+        cps = []
+        for i in range(1, 8):
+            k, cc = i // 2, (c if i % 2 == 0 else oc)
+            cps.append(
+                send(
+                    vsrc.at[s, cc, cut],
+                    vy.at[2 * y + c, cut],
+                    vs.at[0, i - 1],
+                    vr.at[0, i - 1],
+                    dev(z, nxt(y, k), cc, x),
+                )
+            )
+        vy[2 * y + c, cut] = vsrc[s, c, cut]
+        return cps
+
+    def vsum2(s, n, cps):
+        recv(cps)
+        cut = pl.ds(0, n)
+        if s == 0:
+            total = vy[0, cut]
+            for i in range(1, 8):
+                total = total + vy[i, cut]
+        else:
+            total = ((vw[0] + vw[1]) + (vw[2] + vw[3]))[None]
+        vz[s, z, c, cut] = total
+        cps = []
+        for i in range(1, 8):
+            k, cc = i // 2, (c if i % 2 == 0 else oc)
+            cps.append(
+                send(
+                    vz.at[s, z, c, cut],
+                    vz.at[s, z, c, cut],
+                    vs.at[1 + s, i - 1],
+                    vr.at[1 + s, i - 1],
+                    dev(nxt(z, k), y, cc, x),
+                )
+            )
+        return cps
+
+    def vsum3(s, cps, where):
+        recv(cps)
+        for cc, n, out in where:
+            vec_ref[out] = (vz[s, 0, cc, n] + vz[s, 1, cc, n]) + (vz[s, 2, cc, n] + vz[s, 3, cc, n])
+
+    def xsum1():
+        cps = []
+        for i in range(1, 8):
+            k, cc = i // 2, (c if i % 2 == 0 else oc)
+            cps.append(
+                send(
+                    vsrc.at[1, cc, 0],
+                    vx.at[2 * x + c],
+                    ws.at[i - 1],
+                    wr.at[i - 1],
+                    dev(z, y, cc, nxt(x, k)),
+                )
+            )
+        vx[2 * x + c] = vsrc[1, c, 0]
+        return cps
+
+    def xsum2(cps):
+        recv(cps)
+        total = vx[0]
+        for i in range(1, 8):
+            total = total + vx[i]
+        vw[y] = total
         return [
-            send(
-                vy.at[s, y, pl.ds(0, n)],
-                vy.at[s, y, pl.ds(0, n)],
-                vs.at[s, k],
-                vr.at[s, k],
-                dev(z, nxt(y, k), c, x),
-            )
+            send(vw.at[y], vw.at[y], ws.at[6 + k], wr.at[6 + k], dev(z, nxt(y, k), c, x))
             for k in range(1, 4)
         ]
-
-    def vsum3(s, n, cps):
-        recv(cps)
-        cut = pl.ds(0, n)
-        vz[s, z, cut] = (vy[s, 0, cut] + vy[s, 1, cut]) + (vy[s, 2, cut] + vy[s, 3, cut])
-        return [
-            send(
-                vz.at[s, z, cut],
-                vz.at[s, z, cut],
-                vs.at[s, 3 + k],
-                vr.at[s, 3 + k],
-                dev(nxt(z, k), y, c, x),
-            )
-            for k in range(1, 4)
-        ]
-
-    def vsum4(s, n, cps):
-        recv(cps)
-        cut = pl.ds(0, n)
-        vfin[s, c, cut] = (vz[s, 0, cut] + vz[s, 1, cut]) + (vz[s, 2, cut] + vz[s, 3, cut])
-        return send(
-            vfin.at[s, c, cut], vfin.at[s, c, cut], vs.at[s, 7], vr.at[s, 7], dev(z, y, oc, x)
-        )
 
     drained = [0]
 
@@ -441,19 +461,38 @@
         drained[0] = len(pending)
 
     parts = range(NF)
+    pairs = [(f, f + 1) for f in range(0, NF, 2)]
+    last = len(pairs) - 1
     g1, g2, g3 = {}, {}, {}
-    for f in parts:
-        g1[0, f] = gather1(0, f)
-    for f in parts:
-        g2[0, f] = gather2(0, f, g1[0, f])
-    for f in parts:
-        g1[1, f] = gather1(1, f)
+    r0, r1, r2, r3 = {}, {}, {}, {}
+
+    def each(step, a, p, into, *before):
+        for f in pairs[p]:
+            into[a, f] = step(a, f, *[b[a, f] for b in before])
+
+    for p in range(last + 1):
+        each(gather1, 0, p, g1)
+    in_og.wait()
+    mixv = dot(table, og[...], 1, 0) * gate_ref[...]
+    mix[...] = mixv
+    gradv = weight * mixv
+    for f in range(NF):
+        for jj in range(2):
+            own[1, f, jj] = gradv[MOST * jj : MOST * jj + MOST, f * F : f * F + F].astype(BF16)
+    in_up = local(up_hbm.at[0], up, loc.at[2])
+    in_down = local(down_hbm.at[0], down, loc.at[3])
+    each(gather1, 1, 0, g1)
+    for p in range(last + 1):
+        each(gather2, 0, p, g2, g1)
+    for p in range(1, last + 1):
+        each(gather1, 1, p, g1)
 
     recv(tabc)
     tabt = tables[...].astype(F32).reshape(64, TOK).T.astype(BF16)
     table_ref[...] = tabt
     invs = []
-    for q in range(4):
+
+    def slot_rows(q):
         sl = slice(16 * q, 16 * q + 16)
         t16 = dot(tables[q], tok[...], 1, 0)
         c16 = t16 - jnp.mean(t16, axis=1, keepdims=True)
@@ -462,13 +501,18 @@
         n64[sl, :] = c16 * i16
         og64[sl, :] = dot(tables[q], og[...], 1, 0).astype(BF16)
 
-    for f in parts:
-        g3[0, f] = gather3(0, f, g2[0, f])
-        g2[1, f] = gather2(1, f, g1[1, f])
+    slot_rows(0)
+    each(gather2, 1, 0, g2, g1)
+    for q in range(1, 4):
+        slot_rows(q)
+    for p in range(last + 1):
+        each(gather3, 0, p, g3, g2)
+        if p > 0:
+            each(gather2, 1, p, g2, g1)
     in_up.wait()
     for f in parts:
         rows_ready(0, f, g3[0, f])
-        acc = dot(rowmat[0, :, f * F : f * F + F], up[f * F : f * F + F, :], 1, 0)
+        acc = dot(rowmat0[:, f * F : f * F + F], up[f * F : f * F + F, :], 1, 0)
         pre[...] = acc if f == 0 else pre[...] + acc
     prev = pre[...]
     tang = jnp.tanh(GELU_C * (prev + 0.044715 * prev * prev * prev))
@@ -476,39 +520,63 @@
     pre[...] = 0.5 * (1.0 + tang) + 0.5 * prev * (1.0 - tang * tang) * GELU_C * (
         1.0 + 3.0 * 0.044715 * prev * prev
     )
-    outs = [local(rowmat.at[0], rows_hbm, loc.at[4]), local(act, act_hbm, loc.at[5])]
     in_down.wait()
-    r0, r1, r2, r3 = {}, {}, {}, {}
-    for f in parts:
-        r0[0, f] = partial(0, f)
-    for f in parts:
-        g3[1, f] = gather3(1, f, g2[1, f])
-    for f in parts:
-        r1[0, f] = return1(0, f, r0[0, f])
-    for f in parts:
-        rows_ready(1, f, g3[1, f])
-        acc = dot(rowmat[1, :, f * F : f * F + F], down[:, f * F : f * F + F], 1, 1)
-        gact[...] = acc if f == 0 else gact[...] + acc
+    for p in range(last + 1):
+        each(partial, 0, p, r0)
+    each(gather3, 1, 0, g3, g2)
+    for p in range(last + 1):
+        each(return1, 0, p, r1, r0)
+    for p in range(last + 1):
+        if p > 0:
+            each(gather3, 1, p, g3, g2)
+        for f in pairs[p]:
+            rows_ready(1, f, g3[1, f])
+            acc = dot(rowmat1[:, f * F : f * F + F], down[:, f * F : f * F + F], 1, 1)
+            gact[...] = acc if f == 0 else gact[...] + acc
     gpre[...] = (gact[...] * pre[...]).astype(BF16)
-    outs += [local(rowmat.at[1], grads_hbm, loc.at[6]), local(gpre, gp_hbm, loc.at[7])]
-    for f in parts:
-        r0[1, f] = partial(1, f)
-    for f in parts:
-        r2[0, f] = return2(0, f, r1[0, f])
-    for f in parts:
-        r1[1, f] = return1(1, f, r0[1, f])
+    for p in range(last + 1):
+        each(partial, 1, p, r0)
+    for p in range(last + 1):
+        each(return2, 0, p, r2, r1)
+        each(return1, 1, p, r1, r0)
     grad_w = jnp.zeros((2 * MOST, 1), F32)
-    for f in parts:
-        rows = return3(0, f, r2[0, f])
-        grad_w = grad_w + jnp.sum(rows * mix[:, f * F : f * F + F], axis=1, keepdims=True)
-        r3[0, f] = to_x(0, f, rows * weight)
+    for p in range(last + 1):
+        for f in pairs[p]:
+            rows = return3(0, f, r2[0, f])
+            grad_w = grad_w + jnp.sum(rows * mix[:, f * F : f * F + F], axis=1, keepdims=True)
+            r3[0, f] = to_x(0, f, rows * weight)
+        if p < last:
+            each(return2, 1, p, r2, r1)
     grad_logit = grad_w * weight * (1.0 - weight)
-    for f in parts:
-        r2[1, f] = return2(1, f, r1[1, f])
     hg = hid16[...].astype(F32) * grad_logit
     spread(jnp.sum(hg[:MOST], axis=0, keepdims=True), 0, 0, 1)
     spread(jnp.sum(hg[MOST:], axis=0, keepdims=True), 0, 1, 0)
     vsrc[0, 1, 1] = jnp.zeros((8, TILE), F32)
+    each(return2, 1, last, r2, r1)
+    drain()
+    sums1, sums2 = [], []
+
+    def back_rows(f):
+        rows = return3(1, f, r2[1, f])
+        add = [
+            grad_logit[MOST * jj : MOST * jj + MOST]
+            * router_ref[jj : jj + 1, f * F : f * F + F].astype(F32)
+            for jj in range(2)
+        ]
+        rows = rows + jnp.concatenate(add, axis=0)
+        sums1.append(jnp.sum(rows, axis=0, keepdims=True))
+        sums2.append(jnp.sum(rows * n16[:, f * F : f * F + F], axis=0, keepdims=True))
+        return rows
+
+    for p in range(last):
+        for f in pairs[p]:
+            r3[1, f] = to_x(1, f, back_rows(f))
+    ends = [back_rows(f) for f in pairs[last]]
+    spread(jnp.concatenate(sums1, axis=1), 1, 0, 0)
+    spread(jnp.concatenate(sums2, axis=1), 1, 1, 0)
+    wa = xsum1()
+    for f, rows in zip(pairs[last], ends):
+        r3[1, f] = to_x(1, f, rows)
     sums = []
     for f in parts:
         cols = slice(f * F, f * F + F)
@@ -518,97 +586,90 @@
         x64[:, cols] = outrows.astype(BF16)
     spread(jnp.concatenate(sums, axis=1), 0, 0, 0)
     va = vsum1(0, 2)
-    outs += [local(x64, mixrows_hbm, loc.at[8])]
-    drain()
-    for f in parts:
-        rows = return3(1, f, r2[1, f])
-        add = [
-            grad_logit[MOST * jj : MOST * jj + MOST]
-            * router_ref[jj : jj + 1, f * F : f * F + F].astype(F32)
-            for jj in range(2)
-        ]
-        r3[1, f] = to_x(1, f, rows + jnp.concatenate(add, axis=0))
+    wb = xsum2(wa)
     vb = vsum2(0, 2, va)
+    wc = vsum2(1, 1, wb)
     m1 = jnp.zeros((64, 1), F32)
     m2 = jnp.zeros((64, 1), F32)
-    sums, sums_n = [], []
     for f in parts:
         cols = slice(f * F, f * F + F)
         recv(r3[1, f])
         gh = slots[1, f].astype(F32).reshape(64, F)
         ghn = gh * n64[:, cols]
-        sums.append(jnp.sum(gh, axis=0, keepdims=True))
-        sums_n.append(jnp.sum(ghn, axis=0, keepdims=True))
         one = 1.0 + scale_ref[:, cols]
         g64[:, cols] = gh * one
         m1 = m1 + jnp.sum(gh * one, axis=1, keepdims=True)
         m2 = m2 + jnp.sum(ghn * one, axis=1, keepdims=True)
-    spread(jnp.concatenate(sums, axis=1), 1, 0, 0)
-    spread(jnp.concatenate(sums_n, axis=1), 1, 1, 0)
-    wa = vsum1(1, 1)
-    vc = vsum3(0, 2, vb)
-    wb = vsum2(1, 1, wa)
     m1 = m1 * (1.0 / D)
     m2 = m2 * (1.0 / D)
     for q in range(4):
         sl = slice(16 * q, 16 * q + 16)
         c64[sl, :] = (invs[q] * (g64[sl, :] - m1[sl] - n64[sl, :] * m2[sl])).astype(BF16)
-    outs += [local(c64, corr_hbm, loc.at[9])]
-    vd = vsum4(0, 2, vc)
-    wc = vsum3(1, 1, wb)
+    vsum3(0, vb, [(0, 0, 2), (0, 1, 3), (1, 0, 4)])
     drain()
-    vd.wait_recv()
-    vec_ref[2] = vfin[0, 0, 0]
-    vec_ref[3] = vfin[0, 0, 1]
-    vec_ref[4] = vfin[0, 1, 0]
-    wd = vsum4(1, 1, wc)
-    for cp in outs:
-        cp.wait()
-    wd.wait_recv()
-    vec_ref[0] = vfin[1, 0, 0]
-    vec_ref[1] = vfin[1, 1, 0]
-    drain()
+    vsum3(1, wc, [(0, 0, 0), (1, 0, 1)])
 
 
 def finish_kernel(
-    rows_ref,
-    grads_ref,
-    act_ref,
-    gp_ref,
-    tok_ref,
-    og_ref,
+    rows,
+    grads,
+    act,
+    gp,
+    mixrows,
+    corr,
+    tok,
+    og,
+    table_ref,
+    vec_ref,
     gate_ref,
-    table_ref,
-    mixrows_ref,
-    corr_ref,
-    vec_ref,
-    up_ref,
-    down_ref,
-    block_ref,
-    tgrad_ref,
+    up_hbm,
+    down_hbm,
+    block_hbm,
+    tgrad_hbm,
     shift_ref,
     scale_ref,
     ggrad_ref,
     router_ref,
+    up,
+    down,
+    block,
+    tgrad,
+    act_t,
+    sem_out,
 ):
-    up_ref[0] = dot(rows_ref[...], gp_ref[...], 0, 0).astype(BF16)
-    down_ref[0] = dot(act_ref[...], grads_ref[...], 0, 0).astype(BF16)
-    block_ref[...] = (
-        tok_ref[...].astype(F32) + gate_ref[...] * dot(table_ref[...], mixrows_ref[...], 1, 0)
-    ).astype(BF16)
-    tgrad_ref[...] = (
-        og_ref[...].astype(F32) + dot(table_ref[...], corr_ref[...], 1, 0)
-    ).astype(BF16)
-
-    @pl.when(pl.program_id(0) == 0)
-    def _():
-        for i in range(D // TILE):
-            cols = slice(i * TILE, i * TILE + TILE)
-            shift_ref[:, cols] = vec_ref[0, i : i + 1, :]
-            scale_ref[:, cols] = vec_ref[1, i : i + 1, :]
-            ggrad_ref[:, cols] = vec_ref[2, i : i + 1, :]
-            router_ref[0:1, cols] = vec_ref[3, i : i + 1, :]
-            router_ref[1:2, cols] = vec_ref[4, i : i + 1, :]
+    steps = D // STEP
+    for i in range(D // TILE):
+        cols = slice(i * TILE, i * TILE + TILE)
+        shift_ref[:, cols] = vec_ref[0, i : i + 1, :]
+        scale_ref[:, cols] = vec_ref[1, i : i + 1, :]
+        ggrad_ref[:, cols] = vec_ref[2, i : i + 1, :]
+        router_ref[0:1, cols] = vec_ref[3, i : i + 1, :]
+        router_ref[1:2, cols] = vec_ref[4, i : i + 1, :]
+    act_t[...] = act[...].astype(F32).T.astype(BF16)
+    stores = []
+
+    def store(src, dst, sem):
+        cp = pltpu.make_async_copy(src, dst, sem)
+        cp.start()
+        stores.append(cp)
+
+    for t in range(steps):
+        cols = pl.ds(t * STEP, STEP)
+        up[cols, :] = dot(rows[:, cols], gp[...], 0, 0).astype(BF16)
+        store(up.at[cols], up_hbm.at[0, cols], sem_out.at[t, 0])
+        down[:, cols] = dot(act_t[...], grads[:, cols], 1, 0).astype(BF16)
+        store(down.at[:, cols], down_hbm.at[0, :, cols], sem_out.at[t, 1])
+        block[:, cols] = (
+            tok[:, cols].astype(F32)
+            + gate_ref[:, cols] * dot(table_ref[...], mixrows[:, cols], 1, 0)
+        ).astype(BF16)
+        store(block.at[:, cols], block_hbm.at[:, cols], sem_out.at[t, 2])
+        tgrad[:, cols] = (
+            og[:, cols].astype(F32) + dot(table_ref[...], corr[:, cols], 1, 0)
+        ).astype(BF16)
+        store(tgrad.at[:, cols], tgrad_hbm.at[:, cols], sem_out.at[t, 3])
+    for cp in stores:
+        cp.wait()
 
 
 def per_device(tokens, shift, scale, gate, router, up, down, picks, out_grad):
@@ -616,33 +677,31 @@
     vmem = pl.BlockSpec(memory_space=pltpu.VMEM)
     dma = pltpu.SemaphoreType.DMA
     shape = jax.ShapeDtypeStruct
-    rows, grads, act, gp, mixrows, corr, table, vec = pl.pallas_call(
+    vm = pltpu.VMEM
+    *kept, table, vec = pl.pallas_call(
         exchange_kernel,
         out_shape=(
-            shape((SLOTS, D), BF16),
-            shape((SLOTS, D), BF16),
-            shape((SLOTS, HU), BF16),
-            shape((SLOTS, HU), BF16),
-            shape((64, D), BF16),
-            shape((64, D), BF16),
-            shape((TOK, 64), BF16),
-            shape((5, 8, TILE), F32),
+            vm((SLOTS, D), BF16),
+            vm((SLOTS, D), BF16),
+            vm((SLOTS, HU), BF16),
+            vm((SLOTS, HU), BF16),
+            vm((64, D), BF16),
+            vm((64, D), BF16),
+            vm((TOK, D), BF16),
+            vm((TOK, D), BF16),
+            vm((TOK, 64), BF16),
+            vm((5, 8, TILE), F32),
         ),
         in_specs=[hbm, hbm, vmem, vmem, vmem, vmem, hbm, hbm, vmem],
-        out_specs=(hbm, hbm, hbm, hbm, hbm, hbm, vmem, vmem),
+        out_specs=(vmem,) * 10,
         scratch_shapes=[
-            pltpu.VMEM((TOK, D), BF16),
-            pltpu.VMEM((TOK, D), BF16),
             pltpu.VMEM((D, HU), BF16),
             pltpu.VMEM((HU, D), BF16),
             pltpu.VMEM((2, NF, 2, MOST, F), BF16),
             pltpu.VMEM((2, NF, 2, 4, 4, MOST, F), BF16),
             pltpu.VMEM((2, NF // 2, 4, 2, MOST, F), BF16),
-            pltpu.VMEM((2, SLOTS, D), BF16),
             pltpu.VMEM((SLOTS, HU), F32),
             pltpu.VMEM((SLOTS, HU), F32),
-            pltpu.VMEM((SLOTS, HU), BF16),
-            pltpu.VMEM((SLOTS, HU), BF16),
             pltpu.VMEM((2, NF, 2, 4, 4, MOST, F), BF16),
             pltpu.VMEM((2, NF, 4, 4, MOST, F), BF16),
             pltpu.VMEM((2, NF, 3, 4, MOST, F), BF16),
@@ -656,14 +715,13 @@
             pltpu.VMEM((64, D), F32),
             pltpu.VMEM((64, D), BF16),
             pltpu.VMEM((64, D), F32),
-            pltpu.VMEM((64, D), BF16),
-            pltpu.VMEM((64, D), BF16),
+            pltpu.VMEM((2 * MOST, D), F32),
             pltpu.VMEM((2, 2, 2, 8, TILE), F32),
-            pltpu.VMEM((2, 2, 8, TILE), F32),
-            pltpu.VMEM((2, 4, 2, 8, TILE), F32),
-            pltpu.VMEM((2, 4, 2, 8, TILE), F32),
-            pltpu.VMEM((2, 2, 2, 8, TILE), F32),
-            dma((10,)),
+            pltpu.VMEM((8, 2, 8, TILE), F32),
+            pltpu.VMEM((8, 8, TILE), F32),
+            pltpu.VMEM((4, 8, TILE), F32),
+            pltpu.VMEM((2, 4, 2, 2, 8, TILE), F32),
+            dma((4,)),
             dma((3,)),
             dma((3,)),
             dma((2, NF, 3)),
@@ -680,11 +738,13 @@
             dma((2, NF, 3)),
             dma((2, NF, 3)),
             dma((2, NF, 3)),
-            dma((2, 8)),
-            dma((2, 8)),
+            dma((3, 7)),
+            dma((3, 7)),
+            dma((10,)),
+            dma((10,)),
         ],
         compiler_params=pltpu.CompilerParams(
-            collective_id=0, has_side_effects=True, vmem_limit_bytes=56 * 2**20
+            collective_id=0, has_side_effects=True, vmem_limit_bytes=55 * 2**20
         ),
         cost_estimate=pl.CostEstimate(
             flops=12 * SLOTS * D * HU, bytes_accessed=24 * 2**20, transcendentals=SLOTS * HU
@@ -700,13 +760,9 @@
         down,
         picks[0],
     )
-    steps = D // TILE
-    one = lambda i: (0, 0)
-    col = lambda i: (0, i)
-    vecs = pl.BlockSpec((1, D), one)
+    kept = [pltpu.with_memory_space_constraint(a, vm) for a in (*kept, table, vec)]
     up_grad, down_grad, block, tgrad, shift_g, scale_g, gate_g, router_g = pl.pallas_call(
         finish_kernel,
-        grid=(steps,),
         out_shape=(
             shape((1, D, HU), BF16),
             shape((1, HU, D), BF16),
@@ -717,33 +773,21 @@
             shape((1, D), F32),
             shape((2, D), F32),
         ),
-        in_specs=[
-            pl.BlockSpec((SLOTS, TILE), col),
-            pl.BlockSpec((SLOTS, TILE), col),
-            pl.BlockSpec((SLOTS, HU), one),
-            pl.BlockSpec((SLOTS, HU), one),
-            pl.BlockSpec((TOK, TILE), col),
-            pl.BlockSpec((TOK, TILE), col),
-            pl.BlockSpec((1, TILE), col),
-            pl.BlockSpec((TOK, 64), one),
-            pl.BlockSpec((64, TILE), col),
-            pl.BlockSpec((64, TILE), col),
-            pl.BlockSpec((5, 8, TILE), lambda i: (0, 0, 0)),
+        in_specs=[vmem] * 11,
+        out_specs=(hbm, hbm, hbm, hbm, vmem, vmem, vmem, vmem),
+        scratch_shapes=[
+            vm((D, HU), BF16),
+            vm((HU, D), BF16),
+            vm((TOK, D), BF16),
+            vm((TOK, D), BF16),
+            vm((HU, SLOTS), BF16),
+            dma((D // STEP, 4)),
         ],
-        out_specs=(
-            pl.BlockSpec((1, TILE, HU), lambda i: (0, i, 0)),
-            pl.BlockSpec((1, HU, TILE), lambda i: (0, 0, i)),
-            pl.BlockSpec((TOK, TILE), col),
-            pl.BlockSpec((TOK, TILE), col),
-            vecs,
-            vecs,
-            vecs,
-            pl.BlockSpec((2, D), one),
+        compiler_params=pltpu.CompilerParams(vmem_limit_bytes=44 * 2**20),
+        cost_estimate=pl.CostEstimate(
+            flops=4 * SLOTS * D * HU, bytes_accessed=10 * 2**20, transcendentals=0
         ),
-        cost_estimate=pl.CostEstimate(
-            flops=4 * SLOTS * D * HU, bytes_accessed=18 * 2**20, transcendentals=0
-        ),
-    )(rows, grads, act, gp, tokens, out_grad, gate.reshape(1, D), table, mixrows, corr, vec)
+    )(*kept, gate.reshape(1, D))
     return (
         block,
         tgrad,

time: 83 us -> 72.5 us (0.87)
  Pallas kernels: 82 us -> 71.5 us
    pallas_call x2, Pallas kernels: 82 us -> 71.5 us  [the longest x1 66.3 us: per_device(): pl.pallas_call(exchange_kernel, out_shape=(vm((SLOTS, D), BF16), vm((SLOT...]
where the time goes in v3:
time: 72.5 us; the launch traced here: 72.3 us
  Pallas kernels  71.5 us (99%)
  between operations  0.82 us (1%)
    pallas_call x1, Pallas kernels, per_device(): pl.pallas_call(exchange_kernel, out_shape=(vm((SLOTS, D), BF16), vm((SLOT...  66.3 us
    pallas_call x1, Pallas kernels, per_device(): pl.pallas_call(finish_kernel, out_shape=(shape((1, D, HU), BF16), shape((...  5.16 us

profile of v3, /device:TPU:1, one launch (start us, length us, event | category | flops | bytes accessed | tf_op | source)
XLA Modules:
  0.0 72.3 jit_solution(12262155392718126494)
XLA Ops:
  0.6 0.0 copy-start
  0.6 66.3 %shard_map.152 = (bf16[256,4096]{1,0:T(8,128)(2,1)S(1)}, bf16[256,4096]{1,0:T(8,128)(2,1)S(1)}, bf16[256,512]{1,0:T(8,128)(2,1)S(1)}, bf16[256,512]{1,0:T(8,128)...) custom-call(bf16[128,4096]{1,0:T(8,128)(2,1)} %tok_hbm.1, ...), custom_call_target="tpu_custom_call" | custom-call | flops 6442450944 | bytes 25165824 | tf_op jit(solution)/shard_map/pallas_call | solution.py:681
  67.0 0.0 copy-done
  67.0 5.2 %shard_map.153 = (bf16[1,4096,512]{2,1,0:T(8,128)(2,1)}, bf16[1,512,4096]{2,1,0:T(8,128)(2,1)}, bf16[128,4096]{1,0:T(8,128)(2,1)}, bf16[128,4096]{1,0:T(8,128)(2...) custom-call(bf16[256,4096]{1,0:T(8,128)(2,1)S(1)} %get-tuple-element.26.rows, ...), custom_call_target="tpu_custom_call" | custom-call | flops 2147483648 | bytes 10485760 | tf_op jit(solution)/shard_map/pallas_call | solution.py:764
Async XLA Ops:
  0.6 66.3 %copy-start = (f32[4096]{0:T(1024)S(1)}, f32[4096]{0:T(1024)}, u32[]{:S(2)}) copy-start(f32[4096]{0:T(1024)} %param.12) | copy-start | bytes 49156

commit v4 on v3

--- a/solution.py
+++ b/solution.py
@@ -406,17 +406,18 @@
                 total = total + vy[i, cut]
         else:
             total = ((vw[0] + vw[1]) + (vw[2] + vw[3]))[None]
-        vz[s, z, c, cut] = total
+        at = z if s == 0 else x
+        vz[s, at, c, cut] = total
         cps = []
         for i in range(1, 8):
             k, cc = i // 2, (c if i % 2 == 0 else oc)
             cps.append(
                 send(
-                    vz.at[s, z, c, cut],
-                    vz.at[s, z, c, cut],
+                    vz.at[s, at, c, cut],
+                    vz.at[s, at, c, cut],
                     vs.at[1 + s, i - 1],
                     vr.at[1 + s, i - 1],
-                    dev(nxt(z, k), y, cc, x),
+                    dev(nxt(z, k), y, cc, x) if s == 0 else dev(z, y, cc, nxt(x, k)),
                 )
             )
         return cps
@@ -433,13 +434,13 @@
             cps.append(
                 send(
                     vsrc.at[1, cc, 0],
-                    vx.at[2 * x + c],
+                    vx.at[2 * y + c],
                     ws.at[i - 1],
                     wr.at[i - 1],
-                    dev(z, y, cc, nxt(x, k)),
+                    dev(z, nxt(y, k), cc, x),
                 )
             )
-        vx[2 * x + c] = vsrc[1, c, 0]
+        vx[2 * y + c] = vsrc[1, c, 0]
         return cps
 
     def xsum2(cps):
@@ -447,9 +448,9 @@
         total = vx[0]
         for i in range(1, 8):
             total = total + vx[i]
-        vw[y] = total
+        vw[z] = total
         return [
-            send(vw.at[y], vw.at[y], ws.at[6 + k], wr.at[6 + k], dev(z, nxt(y, k), c, x))
+            send(vw.at[z], vw.at[z], ws.at[6 + k], wr.at[6 + k], dev(nxt(z, k), y, c, x))
             for k in range(1, 4)
         ]
 
@@ -509,11 +510,12 @@
         each(gather3, 0, p, g3, g2)
         if p > 0:
             each(gather2, 1, p, g2, g1)
-    in_up.wait()
-    for f in parts:
-        rows_ready(0, f, g3[0, f])
-        acc = dot(rowmat0[:, f * F : f * F + F], up[f * F : f * F + F, :], 1, 0)
-        pre[...] = acc if f == 0 else pre[...] + acc
+        else:
+            in_up.wait()
+        for f in pairs[p]:
+            rows_ready(0, f, g3[0, f])
+            acc = dot(rowmat0[:, f * F : f * F + F], up[f * F : f * F + F, :], 1, 0)
+            pre[...] = acc if f == 0 else pre[...] + acc
     prev = pre[...]
     tang = jnp.tanh(GELU_C * (prev + 0.044715 * prev * prev * prev))
     act[...] = (0.5 * prev * (1.0 + tang)).astype(BF16)
@@ -536,9 +538,11 @@
     gpre[...] = (gact[...] * pre[...]).astype(BF16)
     for p in range(last + 1):
         each(partial, 1, p, r0)
+    each(return2, 0, 0, r2, r1)
     for p in range(last + 1):
+        each(return1, 1, p, r1, r0)
+    for p in range(1, last + 1):
         each(return2, 0, p, r2, r1)
-        each(return1, 1, p, r1, r0)
     grad_w = jnp.zeros((2 * MOST, 1), F32)
     for p in range(last + 1):
         for f in pairs[p]:

time: 72.5 us -> 70.7 us (0.975)
  Pallas kernels: 71.5 us -> 69.7 us
    pallas_call x1, Pallas kernels: 66.3 us -> 64.6 us  [per_device(): pl.pallas_call(exchange_kernel, out_shape=(vm((SLOTS, D), BF16), vm((SLOT...]
where the time goes in v4:
time: 70.7 us; the launch traced here: 70.5 us
  Pallas kernels  69.7 us (99%)
  between operations  0.82 us (1%)
    pallas_call x1, Pallas kernels, per_device(): pl.pallas_call(exchange_kernel, out_shape=(vm((SLOTS, D), BF16), vm((SLOT...  64.6 us
    pallas_call x1, Pallas kernels, per_device(): pl.pallas_call(finish_kernel, out_shape=(shape((1, D, HU), BF16), shape((...  5.17 us

profile of v4, /device:TPU:1, one launch (start us, length us, event | category | flops | bytes accessed | tf_op | source)
XLA Modules:
  0.0 70.5 jit_solution(126549783288221167)
XLA Ops:
  0.6 0.0 copy-start
  0.6 64.6 %shard_map.152 = (bf16[256,4096]{1,0:T(8,128)(2,1)S(1)}, bf16[256,4096]{1,0:T(8,128)(2,1)S(1)}, bf16[256,512]{1,0:T(8,128)(2,1)S(1)}, bf16[256,512]{1,0:T(8,128)...) custom-call(bf16[128,4096]{1,0:T(8,128)(2,1)} %tok_hbm.1, ...), custom_call_target="tpu_custom_call" | custom-call | flops 6442450944 | bytes 25165824 | tf_op jit(solution)/shard_map/pallas_call | solution.py:685
  65.2 0.0 copy-done
  65.2 5.2 %shard_map.153 = (bf16[1,4096,512]{2,1,0:T(8,128)(2,1)}, bf16[1,512,4096]{2,1,0:T(8,128)(2,1)}, bf16[128,4096]{1,0:T(8,128)(2,1)}, bf16[128,4096]{1,0:T(8,128)(2...) custom-call(bf16[256,4096]{1,0:T(8,128)(2,1)S(1)} %get-tuple-element.26.rows, ...), custom_call_target="tpu_custom_call" | custom-call | flops 2147483648 | bytes 10485760 | tf_op jit(solution)/shard_map/pallas_call | solution.py:768
Async XLA Ops:
  0.6 64.6 %copy-start = (f32[4096]{0:T(1024)S(1)}, f32[4096]{0:T(1024)}, u32[]{:S(2)}) copy-start(f32[4096]{0:T(1024)} %param.12) | copy-start | bytes 49156
